TPU v7x, 512 devices: a whole 4x4x16 slice. The times are simulated.
512 devices in a mesh: shift: 8 (over y, x_hi), dom: 32 (over x_lo, z), eh: 2 (over core).
Axes of the slice: x: 4 (x_hi: 2, x_lo: 2; x = x_hi * 2 + x_lo), y: 4, z: 16, core: 2. Of those that a mesh axis runs over, the one named last changes fastest.
Arguments:
- right_side: float32 [2, 512, 32, 128], P('eh', 'dom'), may hold values from -6 to 6
- shifts: float32 [8, 2], P('shift'), may hold values from 0.3 to 1.5
- quad_weights: float32 [8, 2], P('shift'), may hold values from -4 to 4
- hop_table: float32 [8, 2, 64, 64], replicated, may hold values from -0.3125 to 0.3125
- pair_table: float32 [4, 2, 64, 64], replicated, may hold values from -0.5 to 0.5
- hop_type: int32 [512, 3], P('dom'), may hold values from 0 to 7
- pair_type: int32 [512], P('dom'), may hold values from 0 to 3
Outputs:
- filtered: float32 [2, 512, 32, 128], P('eh', ('dom', 'shift'))
All inputs are finite; a program needn't handle non-finite values.
Results may differ from a plain program's by a relative error of at most 0.0003.
Values sent between devices are 32-bit elements; how exact they have to be, the bound alone decides.
No kernel may reach another device: no remote copies, remote signals or barrier semaphores. Data moves between devices by JAX's collectives and lax.ppermute only.
A program may use at most 64 MiB of HBM per device.

v0:
```python
import jax
import jax.numpy as jnp
from jax import lax
from jax.sharding import PartitionSpec as P

ITERS = 2


def shifted(x, axis, by):
    count = lax.axis_size(axis)
    pairs = [(i, i + by) for i in range(count) if 0 <= i + by < count]
    return lax.ppermute(x, axis, pairs)


def extended(x, sides, width):
    for axis, dim in sides:
        count, length = (lax.axis_size(axis), x.shape[dim])
        up = [(i, (i + 1) % count) for i in range(count - 1)]
        down = [(j, i) for i, j in up]
        last = lax.slice_in_dim(x, length - width, length, axis=dim)
        first = lax.slice_in_dim(x, 0, width, axis=dim)
        before = lax.ppermute(last, axis, up)
        after = lax.ppermute(first, axis, down)
        x = jnp.concatenate([before, x, after], axis=dim)
    return x


def from_partner(value, axis, distance):
    mask = 2**distance
    pairs = [(source, source ^ mask) for source in range(lax.axis_size(axis))]
    return lax.ppermute(value, axis, pairs)


def flip(mats):
    return jnp.swapaxes(mats, -1, -2)


def real_form(real_part, imag_part):
    upper = jnp.concatenate([flip(real_part), flip(imag_part)], -1)
    lower = jnp.concatenate([-flip(imag_part), flip(real_part)], -1)
    return jnp.concatenate([upper, lower], -2)


def band_mul(vec, mats):
    return jnp.einsum("phbcj,bji->phbci", vec, mats, precision=lax.Precision.HIGHEST)


def cscale(coef, vec):
    orb = vec.shape[-1] // 2
    coef_re = coef[0][:, None, None, :, None]
    coef_im = coef[1][:, None, None, :, None]
    vec_re, vec_im = (vec[..., :orb], vec[..., orb:])
    return jnp.concatenate(
        [coef_re * vec_re - coef_im * vec_im, coef_re * vec_im + coef_im * vec_re], -1
    )


def cdiv(left, right):
    denom = jnp.maximum(right[0] * right[0] + right[1] * right[1], 1.0)
    return jnp.stack(
        [
            (left[0] * right[0] + left[1] * right[1]) / denom,
            (left[1] * right[0] - left[0] * right[1]) / denom,
        ]
    )


def bilinear(left, right):
    orb = left.shape[-1] // 2
    lre, lim = (left[..., :orb], left[..., orb:])
    rre, rim = (right[..., :orb], right[..., orb:])
    real_sum = jnp.sum(lre * rre - lim * rim, axis=(1, 2, 4))
    imag_sum = jnp.sum(lre * rim + lim * rre, axis=(1, 2, 4))
    return jnp.stack([real_sum, imag_sum])


def squares(resid):
    return lax.psum(bilinear(resid, resid), ("dom", "eh"))


def curvature(direc, image):
    return lax.psum(bilinear(direc, image), ("dom", "eh"))


def body(right_side, shifts, quad_weights, hop_table, pair_table, hop_type, pair_type):
    hop_re, hop_im = (hop_table[:, 0], hop_table[:, 1])
    pair_re, pair_im = (pair_table[:, 0], pair_table[:, 1])
    onsite = real_form(hop_re + flip(hop_re), hop_im + flip(hop_im))
    forward = real_form(hop_re, hop_im)
    backward = real_form(flip(hop_re), flip(hop_im))
    elec_pair = real_form(pair_re, pair_im)
    hole_pair = real_form(flip(pair_re), flip(pair_im))
    orbits = hop_table.shape[-1]
    plain_sign = jnp.ones((2 * orbits,), jnp.float32)
    conj_sign = jnp.concatenate(
        [jnp.ones((orbits,), jnp.float32), -jnp.ones((orbits,), jnp.float32)]
    )
    blocks = hop_type.shape[0]
    earlier = shifted(hop_type[blocks - 2 :], "dom", 1)
    types_pad = jnp.concatenate([earlier, hop_type], 0)
    on_mats = onsite[hop_type[:, 0]]
    fwd_one = forward[hop_type[:, 1]]
    fwd_two = forward[hop_type[:, 2]]
    bwd_one = backward[types_pad[1 : 1 + blocks, 1]]
    bwd_two = backward[types_pad[0:blocks, 2]]
    electron = lax.axis_index("eh") == 0
    in_sign = jnp.where(electron, plain_sign, conj_sign)[None]
    out_sign = jnp.where(electron, plain_sign, -conj_sign)[None]
    pair_mats = jnp.where(electron, hole_pair, elec_pair)[pair_type]
    in_sign = in_sign[:, None, None, :]
    out_sign = out_sign[:, None, None, :]
    points = shifts.shape[0]
    cols_here = right_side.shape[2]
    zval = jnp.broadcast_to(jnp.transpose(shifts)[:, :, None], (2, points, cols_here))
    wval = jnp.transpose(quad_weights)[:, :, None]
    initial = right_side[None]
    sol = jnp.zeros(initial.shape, jnp.float32)
    resid = initial
    direc = initial
    rho = squares(resid)
    for step in range(ITERS):
        signed = direc * in_sign
        padded = extended(signed, (("dom", 2),), 2)
        total = band_mul(signed, on_mats)
        total = (
            total
            + band_mul(padded[:, :, 3 : 3 + blocks], fwd_one)
            + band_mul(padded[:, :, 4 : 4 + blocks], fwd_two)
        )
        total = (
            total
            + band_mul(padded[:, :, 1 : 1 + blocks], bwd_one)
            + band_mul(padded[:, :, 0:blocks], bwd_two)
        )
        total = total * out_sign
        total = total + from_partner(band_mul(direc, pair_mats), "eh", 0)
        image = cscale(zval, direc) - total
        alpha = cdiv(rho, curvature(direc, image))
        sol = sol + cscale(alpha, direc)
        if step + 1 < ITERS:
            resid = resid - cscale(alpha, image)
            rho_next = squares(resid)
            direc = resid + cscale(cdiv(rho_next, rho), direc)
            rho = rho_next
    weighted = jnp.sum(cscale(wval, sol), axis=0)
    filtered = lax.psum_scatter(weighted, "shift", scatter_dimension=1, tiled=True)
    return filtered


def solution(mesh):
    placed = (
        P("eh", "dom", None, None),
        P("shift", None),
        P("shift", None),
        P(),
        P(),
        P("dom", None),
        P("dom"),
    )
    return jax.shard_map(
        body,
        mesh=mesh,
        in_specs=placed,
        out_specs=P("eh", ("dom", "shift"), None, None),
        check_vma=False,
    )
```

profile of v0, /device:TPU:24, one launch (start us, length us, event | category | flops | bytes accessed | tf_op | source)
XLA Modules:
  0.0 483.8 jit_solution(4086633628704202368)
XLA Ops:
  6.5 0.7 copy-done.31
  7.2 1.0 broadcast_multiply_fusion.1
  8.3 1.4 collective-permute-start
  9.7 0.6 slice.220
  10.3 5.1 %collective-permute-start.1 = (s32[2,3]{0,1:T(4,128)}, s32[2,3]{0,1:T(4,128)}, u32[]{:S(2)}, u32[]{:S(2)}) collective-permute-start(s32[2,3]{0,1:T(4,128)} %slice.220), channel_id=1, source_target_pairs={{0,2},{2,4},{4,6},{6,8},{8,10},{10,12},{12,14},{14,16},{16,18},{18... | collective-permute-start | bytes 80 | tf_op jit(solution)/shard_map/ppermute | solution.py:12
  15.5 3.3 collective-permute-start.2
  19.4 0.6 copy-done.29
  20.3 0.6 gather_fusion.5
  21.2 2.5 convolution_bitcast_fusion.1
  23.7 1.9 collective-permute-start.3
  26.3 0.8 fusion.66
  27.1 0.7 bitcast_negate_fusion
  28.0 0.8 add_bitcast_fusion.1
  29.3 0.6 gather_fusion
  30.0 2.5 fusion.40
  32.7 0.6 copy-done.28
  33.8 1.6 gather_fusion.1
  35.4 0.6 gather_fusion.2
  36.0 0.7 fusion.70
  36.7 0.6 copy-done.27
  37.3 0.6 fusion.69
  37.9 2.1 multiply_subtract_fusion.6
  40.1 0.7 pad_add_fusion
  40.9 1.6 gather_fusion.3
  42.5 1.6 gather_fusion.4
  44.1 2.3 fusion.21
  46.4 1.0 convolution_add_fusion.5
  47.5 1.0 fusion.3
  48.7 2.0 fusion.7
  51.1 111.0 %all-reduce = (f32[2,1,32]{2,1,0:T(1,128)S(1)}, f32[2,1,32]{2,1,0:T(1,128)S(1)}) all-reduce(f32[2,1,32]{2,1,0:T(1,128)S(1)} %get-tuple-element.63, f32[2,1,32]{2,1,0:T(1,128)S(1)} %get-tuple-element.62), channel_id=1, replica_groups=mesh['shift'=8,'dom'=32,'eh'=2] {'dom','eh'}, use_global_device_ids=true, to_apply=%region_5.6 | all-reduce | flops 128 | bytes 1024 | tf_op jit(solution)/shard_map/psum | solution.py:82
  162.7 104.9 %psum.30 = f32[2,1,32]{2,1,0:T(1,128)S(1)} all-reduce(f32[2,1,32]{2,1,0:T(1,128)S(1)} %pad_maximum_fusion.7), channel_id=1, replica_groups=mesh['shift'=8,'dom'=32,'eh'=2] {'dom','eh'}, use_global_device_ids=true, to_apply=%region_8.9 | all-reduce | flops 64 | bytes 512 | tf_op jit(solution)/shard_map/psum | solution.py:78
  267.6 1.0 multiply_subtract_fusion.3
  269.0 1.0 copy-done.4
  270.0 1.7 fusion.41
  271.7 1.7 convolution_bitcast_fusion
  273.5 1.3 collective-permute-start.4
  274.8 4.5 collective-permute-start.5
  279.3 1.9 collective-permute-start.6
  281.3 1.4 multiply_subtract_fusion.2
  282.7 1.0 fusion.14
  283.9 1.0 convolution_add_fusion.2
  284.9 1.0 fusion.1
  286.1 1.0 fusion.11
  287.4 105.2 %psum.31 = f32[2,1,32]{2,1,0:T(1,128)S(1)} all-reduce(f32[2,1,32]{2,1,0:T(1,128)S(1)} %pad_maximum_fusion.8), channel_id=1, replica_groups=mesh['shift'=8,'dom'=32,'eh'=2] {'dom','eh'}, use_global_device_ids=true, to_apply=%region_11.12 | all-reduce | flops 64 | bytes 512 | tf_op jit(solution)/shard_map/psum | solution.py:82
  392.8 0.8 copy-done.20
  393.9 1.4 multiply_subtract_fusion
  395.3 0.8 maximum_bitcast_fusion
  396.1 80.8 %reduce-scatter.2.cloned.1.call-done = f32[1,2,32,128]{3,2,1,0:T(8,128)} async-done(((f32[1,16,32,128]{3,2,1,0:T(8,128)}), f32[1,2,32,128]{3,2,1,0:T(8,128)}) %reduce-scatter.2.cloned.1.call-update) | async-done | bytes 32784 | tf_op jit(solution)/shard_map/reduce_scatter | solution.py:146
  (110 shorter events, 6.2 us)
Async XLA Ops:
  6.5 470.5 %reduce-scatter.2.cloned.1.call-start = ((), (), s32[]{:S(2)}) async-start(), calls=%async_computation.1 | async-start | bytes 294912 | tf_op jit(solution)/shard_map/reduce_scatter | solution.py:146
  6.5 0.7 copy-start.31
  7.2 11.5 %copy-start.24 = (f32[4,2,64,64]{3,2,1,0:T(8,128)S(1)}, f32[4,2,64,64]{3,2,1,0:T(8,128)}, u32[]{:S(2)}) copy-start(f32[4,2,64,64]{3,2,1,0:T(8,128)} %param.11) | copy-start | bytes 393220
  8.2 10.6 %copy-start.8 = (f32[1,1,16,32,128]{4,3,2,1,0:T(8,128)}, f32[1,1,16,32,128]{4,3,2,1,0:T(8,128)S(1)}, u32[]{:S(2)}) copy-start(f32[1,1,16,32,128]{4,3,2,1,0:T(8,128)S(1)} %broadcast_multiply_fusion.1) | copy-start | bytes 786436
  8.2 1.5 copy-start.25
  8.3 38.2 %collective-permute-start = (f32[1,1,2,32,128]{4,3,2,1,0:T(8,128)S(1)}, f32[1,1,2,32,128]{4,3,2,1,0:T(8,128)S(1)}, u32[]{:S(2)}, u32[]{:S(2)}) collective-permute-start(f32[1,1,2,32,128]{4,3,2,1,0:T(8,128)S(1)} %get-tuple-element.41), channel_id=1, source_target_pairs={{2,0},{4,2},{6,4},{8,6},{10,8},{12,10},{14,12},{16,14},{18,16},{20... | collective-permute-start | bytes 98312 | tf_op jit(solution)/shard_map/ppermute | solution.py:23
  10.3 29.7 %collective-permute-start.1 = (s32[2,3]{0,1:T(4,128)}, s32[2,3]{0,1:T(4,128)}, u32[]{:S(2)}, u32[]{:S(2)}) collective-permute-start(s32[2,3]{0,1:T(4,128)} %slice.220), channel_id=1, source_target_pairs={{0,2},{2,4},{4,6},{6,8},{8,10},{10,12},{12,14},{14,16},{16,18},{18... | collective-permute-start | bytes 80 | tf_op jit(solution)/shard_map/ppermute | solution.py:12
  15.5 28.6 %collective-permute-start.2 = (f32[1,1,2,32,128]{4,3,2,1,0:T(8,128)S(1)}, f32[1,1,2,32,128]{4,3,2,1,0:T(8,128)S(1)}, u32[]{:S(2)}, u32[]{:S(2)}) collective-permute-start(f32[1,1,2,32,128]{4,3,2,1,0:T(8,128)S(1)} %get-tuple-element.42), channel_id=1, source_target_pairs={{0,2},{2,4},{4,6},{6,8},{8,10},{10,12},{12,14},{14,16},{16,18},{18... | collective-permute-start | bytes 98312 | tf_op jit(solution)/shard_map/ppermute | solution.py:22
  19.4 0.7 copy-start.29
  20.3 1.0 copy-start
  21.2 4.9 %copy-start.12 = (f32[8,2,64,64]{3,2,1,0:T(8,128)S(1)}, f32[8,2,64,64]{3,2,1,0:T(8,128)}, u32[]{:S(2)}) copy-start(f32[8,2,64,64]{3,2,1,0:T(8,128)} %param.10) | copy-start | bytes 786436
  23.7 24.8 %collective-permute-start.3 = (f32[1,1,16,32,128]{4,3,2,1,0:T(8,128)}, f32[1,1,16,32,128]{4,3,2,1,0:T(8,128)}, u32[]{:S(2)}, u32[]{:S(2)}) collective-permute-start(f32[1,1,16,32,128]{4,3,2,1,0:T(8,128)} %convolution_bitcast_fusion.1), channel_id=1, source_target_pairs={{0,1},{1,0},{2,3},{3,2},{4,5},{5,4},{6,7},{7,6},{8,9},{9,8},{10,11... | collective-permute-start | bytes 786440 | tf_op jit(solution)/shard_map/ppermute | solution.py:31
  26.2 1.7 copy-start.15
  26.3 0.8 copy-start.10
  28.0 0.8 copy-start.13
  28.0 1.1 copy-start.23
  29.9 2.5 copy-start.3
  29.9 2.5 copy-start.16
  30.0 2.5 copy-start.18
  32.5 1.0 copy-start.11
  32.5 1.0 copy-start.14
  32.5 1.1 copy-start.19
  32.7 0.6 copy-start.28
  35.4 0.7 copy-start.26
  36.0 0.7 copy-start.30
  36.7 0.7 copy-start.27
  42.5 1.6 copy-start.9
  44.1 2.4 copy-start.1
  44.1 2.4 copy-start.22
  47.4 1.2 copy-start.5
  47.5 1.3 copy-start.17
  268.7 1.2 copy-start.4
  271.7 11.0 %copy-start.7 = (f32[16,128,128]{2,1,0:T(8,128)S(1)}, f32[16,128,128]{2,1,0:T(8,128)}, u32[]{:S(2)}) copy-start(f32[16,128,128]{2,1,0:T(8,128)} %gather_fusion.3) | copy-start | bytes 3145732
  273.5 10.2 %collective-permute-start.4 = (f32[1,1,2,32,128]{4,3,2,1,0:T(8,128)S(1)}, f32[1,1,2,32,128]{4,3,2,1,0:T(8,128)S(1)}, u32[]{:S(2)}, u32[]{:S(2)}) collective-permute-start(f32[1,1,2,32,128]{4,3,2,1,0:T(8,128)S(1)} %get-tuple-element.35), channel_id=1, source_target_pairs={{2,0},{4,2},{6,4},{8,6},{10,8},{12,10},{14,12},{16,14},{18,16},{20... | collective-permute-start | bytes 98312 | tf_op jit(solution)/shard_map/ppermute | solution.py:23
  274.8 7.9 %collective-permute-start.5 = (f32[1,1,2,32,128]{4,3,2,1,0:T(8,128)S(1)}, f32[1,1,2,32,128]{4,3,2,1,0:T(8,128)S(1)}, u32[]{:S(2)}, u32[]{:S(2)}) collective-permute-start(f32[1,1,2,32,128]{4,3,2,1,0:T(8,128)S(1)} %get-tuple-element.36), channel_id=1, source_target_pairs={{0,2},{2,4},{4,6},{6,8},{8,10},{10,12},{12,14},{14,16},{16,18},{18... | collective-permute-start | bytes 98312 | tf_op jit(solution)/shard_map/ppermute | solution.py:22
  279.3 6.6 %collective-permute-start.6 = (f32[1,1,16,32,128]{4,3,2,1,0:T(8,128)S(1)}, f32[1,1,16,32,128]{4,3,2,1,0:T(8,128)S(1)}, u32[]{:S(2)}, u32[]{:S(2)}) collective-permute-start(f32[1,1,16,32,128]{4,3,2,1,0:T(8,128)S(1)} %convolution_bitcast_fusion), channel_id=1, source_target_pairs={{0,1},{1,0},{2,3},{3,2},{4,5},{5,4},{6,7},{7,6},{8,9},{9,8},{10,11... | collective-permute-start | bytes 786440 | tf_op jit(solution)/shard_map/ppermute | solution.py:31
  282.7 1.2 copy-start.2
  284.9 1.2 copy-start.6
  392.6 1.0 copy-start.20
  392.6 1.0 copy-start.21
Sparse Core Ops, SparseCore 0:
  396.3 80.6 reduce-scatter.1
where the time goes:
time: 485 us; the launch traced here: 484 us
  blocking collectives  321 us (66%)
  waiting for transfers between devices  80.9 us (17%)
  starting transfers between devices  19.5 us (4%)
  matrix products  18.7 us (4%)
  local copies, waits for them, and re-layouts  15.4 us (3%)
  other arithmetic  14.3 us (3%)
  between operations  14 us (3%)
    psum x2, blocking collectives, curvature(): return lax.psum(bilinear(direc, image), ('dom', 'eh'))  216 us
    psum x1, blocking collectives, squares(): return lax.psum(bilinear(resid, resid), ('dom', 'eh'))  105 us
    reduce_scatter x1, waiting for transfers between devices, body(): lax.psum_scatter(weighted, 'shift', scatter_dimension=1, tiled=True)  80.8 us
    dot_general x12, matrix products, band_mul(): jnp.einsum('phbcj,bji->phbci', vec, mats, precision=lax.Precision.HIGHEST)  18.7 us
  transfers between devices with their start and end apart: 8, of which 1 were waited for; matrix products, arithmetic and copies ran while one was open for 6% of the time, Pallas kernels for 0%

commit v1 on v0

v1 whole, which is shorter than its diff:
```python
import jax
import jax.numpy as jnp
from jax import lax
from jax.experimental import pallas as pl
from jax.experimental.pallas import tpu as pltpu
from jax.sharding import PartitionSpec as P

ALL = ("shift", "dom", "eh")
F32 = jnp.float32
BF16 = jnp.bfloat16
SHIFTS, DOMS, EHS = 8, 32, 2
BLK, COLS, LANES = 16, 32, 128
HALF = BLK // 2
WIN = HALF + 6
REACH = HALF + 2
VM = pltpu.CompilerParams(vmem_limit_bytes=48 * 1024 * 1024)


def flat(s, d, e):
    return (s * DOMS + d) * EHS + e


def halo_pairs():
    pairs = []
    for s in range(SHIFTS):
        by = 1 if s < SHIFTS // 2 else -1
        for d in range(DOMS):
            if 0 <= d + by < DOMS:
                pairs += [(flat(s, d, e), flat(s, d + by, e)) for e in range(EHS)]
    return pairs


def moment_groups():
    groups = []
    for turn in range(2):
        for gx in range(2):
            for e in range(EHS):
                group = []
                for d in range(DOMS):
                    z, xl = d % 16, d // 16
                    ylo, yhi = ((1, 2), (0, 3))[turn ^ ((z % 8) // 4)]
                    xh = gx ^ xl
                    group += [flat(ylo * 2 + xh, d, e), flat(yhi * 2 + xh, d, e)]
                groups.append(group)
    return groups


POINT_ROWS = [2 * d + k for d in (0, 4, 16, 20) for k in range(2)]


def halves(shape):
    lane = lax.broadcasted_iota(jnp.int32, shape, len(shape) - 1)
    return jnp.where(lane < LANES // 2, 1.0, -1.0).astype(F32)


def split3(x):
    a = x.astype(BF16)
    r = x - a.astype(F32)
    b = r.astype(BF16)
    c = (r - b.astype(F32)).astype(BF16)
    return a, b, c


def quad(a, b, c, d):
    return jnp.concatenate(
        [jnp.concatenate([a, b], 1), jnp.concatenate([c, d], 1)], 0
    )


def tables_kernel(hop_ref, pair_ref, hop_out, pair_out):
    def put(out, at, mat):
        out[at] = jnp.concatenate(split3(mat), 1)

    for t in range(8):
        re, im = hop_ref[t, 0], hop_ref[t, 1]
        ret, imt = re.T, im.T
        bwd = quad(re, im, -im, re)
        fwd = quad(ret, imt, -imt, ret)
        put(hop_out, 3 * t, fwd)
        put(hop_out, 3 * t + 1, bwd)
        put(hop_out, 3 * t + 2, fwd + bwd)
    for t in range(4):
        re, im = pair_ref[t, 0], pair_ref[t, 1]
        ret, imt = re.T, im.T
        put(pair_out, 2 * t, quad(ret, imt, imt, -ret))
        put(pair_out, 2 * t + 1, quad(-re, im, im, re))


def product(lhs, tabs):
    rows = lhs.shape[0] // 3
    both = jnp.concatenate([t[:, : 2 * LANES] for t in tabs], 0)
    third = jnp.concatenate([t[:, 2 * LANES :] for t in tabs], 0)
    big = jnp.dot(lhs, both, preferred_element_type=F32)
    small = jnp.dot(lhs[:rows], third, preferred_element_type=F32)
    small = small + big[2 * rows :, :LANES] + big[rows : 2 * rows, LANES:]
    small = small + (big[:rows, LANES:] + big[rows : 2 * rows, :LANES])
    return big[:rows, :LANES] + small


def moments_kernel(
    hop_s, pair_s, shift_s, weight_s, both_ref, recv_ref, hop_t, pair_t,
    mom_ref, img_ref, u_ref, us_ref, g_ref, gs_ref, rt_ref, wt_ref, sem,
):
    point, eh = lax.axis_index("shift"), lax.axis_index("eh")
    low = point < SHIFTS // 2
    base = jnp.where(low, 0, HALF)
    types = pltpu.make_async_copy(recv_ref.at[pl.ds(256, 8)], rt_ref, sem)
    types.start()
    sign = halves((1, LANES))

    def load(at, elec, hole):
        u_ref[at, :COLS] = elec
        u_ref[at, COLS:] = hole * sign

    @pl.when(low)
    def _():
        for j in range(2):
            load(j, recv_ref[pl.ds((2 + j) * COLS, COLS)], recv_ref[pl.ds((6 + j) * COLS, COLS)])
        for j in range(12):
            load(2 + j, both_ref[0, j], both_ref[1, j])

    @pl.when(jnp.logical_not(low))
    def _():
        for j in range(10):
            load(j, both_ref[0, 6 + j], both_ref[1, 6 + j])
        for j in range(4):
            load(10 + j, recv_ref[pl.ds(j * COLS, COLS)], recv_ref[pl.ds((4 + j) * COLS, COLS)])

    for j in range(WIN):
        us_ref[j] = jnp.concatenate(split3(u_ref[j]), 0)
    types.wait()
    valid = rt_ref[0, 64]
    for j in range(WIN):
        i = base + (j - 2)
        own = jnp.logical_and(i >= 0, i < BLK)
        at = jnp.bitwise_and(i, BLK - 1)
        for c in range(4):
            here = hop_s[at, c] if c < 3 else pair_s[at]
            there = rt_ref[0, at * 4 + c].astype(jnp.int32)
            wt_ref[j, c] = jnp.where(own, here, there)

    def hop(kind, j, c):
        return hop_t[3 * wt_ref[j, c] + kind]

    def crossed(ref, at, sgn=None):
        zero = jnp.zeros((COLS, LANES), BF16)
        rows = []
        for part in range(3):
            x = ref[at, pl.ds(part * 2 * COLS + COLS, COLS)]
            rows += [x if sgn is None else -x, zero]
        return jnp.concatenate(rows, 0)

    def crossed_up(ref, at):
        zero = jnp.zeros((COLS, LANES), BF16)
        rows = []
        for part in range(3):
            rows += [zero, ref[at, pl.ds(part * 2 * COLS, COLS)]]
        return jnp.concatenate(rows, 0)

    for m in range(REACH):
        j = m + 2
        lhs = jnp.concatenate(
            [us_ref[m + k] for k in range(5)] + [crossed(us_ref, j), crossed_up(us_ref, j)], 1
        )
        tabs = [
            hop(1, j - 2, 2),
            hop(1, j - 1, 1),
            hop(2, j, 0),
            hop(0, j, 1),
            hop(0, j, 2),
            pair_t[2 * wt_ref[j, 3]],
            pair_t[2 * wt_ref[j, 3] + 1],
        ]
        img = product(lhs, tabs)
        if m >= HALF:
            img = jnp.where(jnp.logical_or(low, valid > 0.5), img, 0.0)
        g_ref[m] = img
        gs_ref[m] = jnp.concatenate(split3(img), 0)

    zero = jnp.zeros((2 * COLS, LANES), F32)
    re = [zero] * 4
    im = [zero] * 4
    for m in range(HALF):
        j = m + 2
        lhs = jnp.concatenate([gs_ref[m + k] for k in range(3)] + [crossed(gs_ref, m, -1)], 1)
        tabs = [hop(0, j, 0), hop(0, j, 1), hop(0, j, 2), pair_t[2 * wt_ref[j, 3]]]
        y = product(lhs, tabs)
        u, g = u_ref[j], g_ref[m]
        gr = pltpu.roll(g, LANES // 2, 1)
        for n, (a, b, br) in enumerate(
            ((u, u, pltpu.roll(u, LANES // 2, 1)), (u, g, gr), (g, g, gr), (g, y, pltpu.roll(y, LANES // 2, 1)))
        ):
            re[n] = re[n] + a * b
            im[n] = im[n] + a * br
    ones = jnp.ones((8, LANES), F32)
    rows = []
    for n in range(4):
        s = 1.0 if n in (0, 2) else -1.0
        w = 2.0 if n == 3 else 1.0
        rows.append(w * sign * (re[n][:COLS] + s * re[n][COLS:]))
        rows.append(w * (im[n][:COLS] - s * im[n][COLS:]))
    sums = [
        lax.dot_general(
            ones, jnp.concatenate(rows[4 * k : 4 * k + 4], 0), (((1,), (1,)), ((), ())),
            precision=lax.Precision.HIGHEST, preferred_element_type=F32,
        )
        for k in range(2)
    ]
    lane = lax.broadcasted_iota(jnp.int32, (1, LANES), 1)
    par = jnp.where(lane == 0, shift_s[0, 0], jnp.where(lane == 1, shift_s[0, 1], 0.0))
    par = jnp.where(lane == 2, weight_s[0, 0], jnp.where(lane == 3, weight_s[0, 1], par))
    mine = jnp.concatenate([sums[0][:1], sums[1][:1], par, jnp.zeros_like(par)], 0)
    mom_ref[...] = jnp.broadcast_to(mine[None], mom_ref.shape)
    first = 2 * jnp.bitwise_and(point, 3)
    turn = jnp.where(eh == 0, jnp.ones_like(sign), -sign)
    for k in range(2):
        img_ref[k] = turn * g_ref[first + k, pl.ds(pl.multiple_of(eh * COLS, COLS), COLS)]


def cmul(a, b):
    return a[0] * b[0] - a[1] * b[1], a[0] * b[1] + a[1] * b[0]


def cadd(a, b):
    return a[0] + b[0], a[1] + b[1]


def cdiv(a, b):
    denom = jnp.maximum(b[0] * b[0] + b[1] * b[1], 1.0)
    return (a[0] * b[0] + a[1] * b[1]) / denom, (a[1] * b[0] - a[0] * b[1]) / denom


def combine_kernel(mom_ref, right_ref, img_ref, out_ref):
    total = jnp.sum(mom_ref[...], axis=0)
    pts = jnp.concatenate([mom_ref[j, 2:3] for j in POINT_ROWS], 0)

    def moment(n):
        row = total[n // 2 : n // 2 + 1]
        at = (n % 2) * 64
        return tuple(
            jnp.broadcast_to(row[:, at + k * COLS : at + (k + 1) * COLS], (SHIFTS, COLS))
            for k in range(2)
        )

    def param(n):
        return tuple(
            jnp.broadcast_to(pts[:, n + k : n + k + 1], (SHIFTS, COLS)) for k in range(2)
        )

    m0, m1, m2, m3 = (moment(n) for n in range(4))
    z, w = param(0), param(2)

    def minus(a, b):
        return a[0] - b[0], a[1] - b[1]

    def twice(a):
        return 2.0 * a[0], 2.0 * a[1]

    a0 = cdiv(m0, minus(cmul(z, m0), m1))
    az = cmul(a0, z)
    s = (1.0 - az[0], -az[1])
    s2, sa, aa = cmul(s, s), cmul(s, a0), cmul(a0, a0)
    rho = cadd(cadd(cmul(s2, m0), twice(cmul(sa, m1))), cmul(aa, m2))
    c = cadd(s, cdiv(rho, m0))
    cc, ca = cmul(c, c), cmul(c, a0)
    pp = cadd(cadd(cmul(cc, m0), twice(cmul(ca, m1))), cmul(aa, m2))
    php = cadd(cadd(cmul(cc, m1), twice(cmul(ca, m2))), cmul(aa, m3))
    a1 = cdiv(rho, minus(cmul(z, pp), php))
    c0 = cmul(w, cadd(a0, cmul(a1, c)))
    c1 = cmul(w, cmul(a1, a0))
    rows = [jnp.sum(x, axis=0, keepdims=True) for x in (*c0, *c1)]
    stack = jnp.concatenate(rows + [jnp.zeros((4, COLS), F32)], 0)
    stack = jnp.concatenate([stack, jnp.zeros((8, LANES - COLS), F32)], 1)
    cols = stack.T[:COLS]
    sign = -halves((1, LANES))
    point = lax.axis_index("shift")
    for k in range(2):
        b, g = right_ref[0, 2 * point + k], img_ref[k]
        out = cols[:, 0:1] * b + cols[:, 1:2] * (pltpu.roll(b, LANES // 2, 1) * sign)
        out = out + cols[:, 2:3] * g + cols[:, 3:4] * (pltpu.roll(g, LANES // 2, 1) * sign)
        out_ref[0, k] = out


def body(right_side, shifts, quad_weights, hop_table, pair_table, hop_type, pair_type):
    smem = pl.BlockSpec(memory_space=pltpu.SMEM)
    vmem = pl.BlockSpec(memory_space=pltpu.VMEM)
    low = lax.axis_index("shift") < SHIFTS // 2
    types = jnp.concatenate([hop_type, pair_type[:, None]], 1).astype(F32).reshape(1, 64)
    types = jnp.concatenate([types, jnp.ones((1, 64), F32)], 1)
    both = lax.all_gather(right_side[0], "eh")
    edge = lax.dynamic_slice_in_dim(both, jnp.where(low, BLK - 4, 0), 4, 1)
    payload = jnp.concatenate(
        [edge.reshape(8 * COLS, LANES), jnp.broadcast_to(types, (8, LANES))], 0
    )
    recv = lax.ppermute(payload, ALL, halo_pairs())
    hop_t, pair_t = pl.pallas_call(
        tables_kernel,
        out_shape=[
            jax.ShapeDtypeStruct((24, LANES, 3 * LANES), BF16),
            jax.ShapeDtypeStruct((8, LANES, 3 * LANES), BF16),
        ],
        in_specs=[vmem, vmem],
        out_specs=[vmem, vmem],
        compiler_params=VM,
        name="tables",
    )(hop_table, pair_table)
    mom, img = pl.pallas_call(
        moments_kernel,
        out_shape=[
            jax.ShapeDtypeStruct((2 * DOMS, 4, LANES), F32),
            jax.ShapeDtypeStruct((2, COLS, LANES), F32),
        ],
        in_specs=[smem] * 4 + [vmem] * 4,
        out_specs=[vmem, vmem],
        scratch_shapes=[
            pltpu.VMEM((WIN, 2 * COLS, LANES), F32),
            pltpu.VMEM((WIN, 6 * COLS, LANES), BF16),
            pltpu.VMEM((REACH, 2 * COLS, LANES), F32),
            pltpu.VMEM((REACH, 6 * COLS, LANES), BF16),
            pltpu.SMEM((8, LANES), F32),
            pltpu.SMEM((WIN, 4), jnp.int32),
            pltpu.SemaphoreType.DMA,
        ],
        compiler_params=VM,
        name="moments",
    )(hop_type, pair_type, shifts, quad_weights, both, recv, hop_t, pair_t)
    parts = lax.all_to_all(mom, ALL, 0, 0, axis_index_groups=moment_groups())
    return pl.pallas_call(
        combine_kernel,
        out_shape=jax.ShapeDtypeStruct((1, 2, COLS, LANES), F32),
        in_specs=[vmem, vmem, vmem],
        out_specs=vmem,
        compiler_params=VM,
        name="combine",
    )(parts, right_side, img)


def solution(mesh):
    placed = (
        P("eh", "dom", None, None),
        P("shift", None),
        P("shift", None),
        P(),
        P(),
        P("dom", None),
        P("dom"),
    )
    return jax.shard_map(
        body,
        mesh=mesh,
        in_specs=placed,
        out_specs=P("eh", ("dom", "shift"), None, None),
        check_vma=False,
    )
```

time: 485 us -> 56.7 us (0.12)
  blocking collectives: 321 us -> 39.7 us
  waiting for transfers between devices: 80.9 us -> 2.74 us
  matrix products: 18.7 us -> 0 us
  starting transfers between devices: 19.5 us -> 1.29 us
  between operations: 14 us -> 0.06 us
  other arithmetic: 14.3 us -> 0.72 us
  local copies, waits for them, and re-layouts: 15.4 us -> 4.91 us
  Pallas kernels: 0 us -> 6.23 us
    psum x3 -> x0, blocking collectives: 321 us -> none  [the longest x2 216 us: curvature(): return lax.psum(bilinear(direc, image), ('dom', 'eh'))]
    reduce_scatter x1 -> x0, waiting for transfers between devices: 80.8 us -> none  [body(): lax.psum_scatter(weighted, 'shift', scatter_dimension=1, tiled=True)]
    all_to_all x0 -> x1, blocking collectives: none -> 37.3 us  [body(): parts = lax.all_to_all(mom, ALL, 0, 0, axis_index_groups=moment_groups())]
    dot_general x12 -> x0, matrix products: 18.7 us -> none  [band_mul(): jnp.einsum('phbcj,bji->phbci', vec, mats, precision=lax.Precision.HIGHEST)]
    ppermute x7 -> x1, starting transfers between devices: 19.5 us -> 1.29 us  [body(): recv = lax.ppermute(payload, ALL, halo_pairs())]
    gather x6 -> x0, local copies, waits for them, and re-layouts: 6.6 us -> none  [the longest x1 1.61 us: body(): bwd_two = backward[types_pad[0:blocks, 2]]]
    sub x7 -> x0, other arithmetic: 6.38 us -> none  [the longest x6 6.24 us: cscale(): coef_re * vec_re - coef_im * vec_im]
    pallas_call x0 -> x3, Pallas kernels: none -> 6.23 us  [the longest x1 4.01 us: body(): pl.pallas_call(moments_kernel, out_shape=[jax.ShapeDtypeStruct((2 * DOMS,...]
  transfers between devices with their start and end apart: 8 -> 1, of which waited for: 1 -> 1; matrix products, arithmetic and copies ran while one was open for 6% -> 1% of each run, Pallas kernels for 0% -> 2%
where the time goes in v1:
time: 56.7 us; the launch traced here: 55.6 us
  blocking collectives  39.7 us (70%)
  Pallas kernels  6.23 us (11%)
  local copies, waits for them, and re-layouts  4.91 us (9%)
  waiting for transfers between devices  2.74 us (5%)
  starting transfers between devices  1.29 us (2%)
  other arithmetic  0.72 us (1%)
    all_to_all x1, blocking collectives, body(): parts = lax.all_to_all(mom, ALL, 0, 0, axis_index_groups=moment_groups())  37.3 us
    unnamed x13, local copies, waits for them, and re-layouts  4.72 us
    pallas_call x1, Pallas kernels, body(): pl.pallas_call(moments_kernel, out_shape=[jax.ShapeDtypeStruct((2 * DOMS,...  4.01 us
    ppermute x1, waiting for transfers between devices, body(): recv = lax.ppermute(payload, ALL, halo_pairs())  2.74 us
    all_gather x1, blocking collectives, body(): both = lax.all_gather(right_side[0], 'eh')  2.39 us
    pallas_call x1, Pallas kernels, body(): pl.pallas_call(combine_kernel, out_shape=jax.ShapeDtypeStruct((1, 2, COLS...  1.33 us
    ppermute x1, starting transfers between devices, body(): recv = lax.ppermute(payload, ALL, halo_pairs())  1.29 us
  transfers between devices with their start and end apart: 1, of which 1 were waited for; matrix products, arithmetic and copies ran while one was open for 1% of the time, Pallas kernels for 2%

profile of v1, /device:TPU:24, one launch (start us, length us, event | category | flops | bytes accessed | tf_op | source)
XLA Modules:
  0.0 55.6 jit_solution(11794311251853951744)
XLA Ops:
  0.0 0.7 %add_convert_fusion = f32[16,4]{0,1:T(4,128)S(1)} fusion(s32[16,1]{0,1:T(1,128)} %bitcast.4, s32[16,3]{0,1:T(4,128)} %param.12), kind=kLoop, calls=%fused_computation.1 | loop fusion | flops 128 | bytes 512 | tf_op jit(solution)/shard_map/convert_element_type | solution.py:288
  0.7 0.1 copy.12
  0.8 0.1 convert_element_type.14
  0.9 2.4 %all_gather.3.both_ref = f32[2,16,32,128]{3,2,1,0:T(8,128)S(1)} all-gather(f32[1,16,32,128]{3,2,1,0:T(8,128)} %right_ref.1), channel_id=1, replica_groups=mesh['shift'=8,'dom'=32,'eh'=2] {'eh'}, dimensions={0}, use_global_device_ids=true | all-gather | bytes 786432 | tf_op jit(solution)/shard_map/all_gather | solution.py:290
  3.3 1.3 %collective-permute-start = (f32[264,128]{1,0:T(8,128)S(1)}, f32[264,128]{1,0:T(8,128)S(1)}, u32[]{:S(2)}, u32[]{:S(2)}) collective-permute-start(f32[264,128]{1,0:T(8,128)S(1)} %pad_maximum_fusion), channel_id=1, source_target_pairs={{0,2},{1,3},{2,4},{3,5},{4,6},{5,7},{6,8},{7,9},{8,10},{9,11},{10,... | collective-permute-start | bytes 405512 | tf_op jit(solution)/shard_map/ppermute | solution.py:295
  4.6 0.8 %copy.13.hop_s = s32[16,3]{1,0:T(8,128)S(1)} copy(s32[16,3]{0,1:T(4,128)} %param.12) | data formatting | bytes 384 | tf_op args[5]
  5.4 0.0 copy-start.1
  5.4 1.0 %copy-done.1 = f32[8,2,64,64]{3,2,1,0:T(8,128)S(1)} copy-done((f32[8,2,64,64]{3,2,1,0:T(8,128)S(1)}, f32[8,2,64,64]{3,2,1,0:T(8,128)}, u32[]{:S(2)}) %copy-start.1) | copy-done | bytes 262168
  6.4 0.0 copy-start.2
  6.4 0.9 %copy-done.2 = f32[4,2,64,64]{3,2,1,0:T(8,128)S(1)} copy-done((f32[4,2,64,64]{3,2,1,0:T(8,128)S(1)}, f32[4,2,64,64]{3,2,1,0:T(8,128)}, u32[]{:S(2)}) %copy-start.2) | copy-done | bytes 131096
  7.4 0.0 copy-start
  7.4 0.9 %tables.1 = (bf16[24,128,384]{2,1,0:T(8,128)(2,1)S(1)}, bf16[8,128,384]{2,1,0:T(8,128)(2,1)S(1)}) custom-call(f32[8,2,64,64]{3,2,1,0:T(8,128)S(1)} %copy-done.1, f32[4,2,64,64]{3,2,1,0:T(8,128)S(1)} %copy-done.2), custom_call_target="tpu_custom_call" | custom-call | tf_op jit(solution)/shard_map/tables/pallas_call | solution.py:296
  8.3 2.7 %collective-permute-done.recv_ref = f32[264,128]{1,0:T(8,128)S(1)} collective-permute-done((f32[264,128]{1,0:T(8,128)S(1)}, f32[264,128]{1,0:T(8,128)S(1)}, u32[]{:S(2)}, u32[]{:S(2)}) %collective-permute-start) | collective-permute-done | bytes 135200 | tf_op jit(solution)/shard_map/ppermute | solution.py:295
  11.0 0.0 copy-start.3
  11.0 0.7 %copy-done.3 = s32[16]{0:T(128)S(1)} copy-done((s32[16]{0:T(128)S(1)}, s32[16]{0:T(128)}, u32[]{:S(2)}) %copy-start.3) | copy-done | bytes 88
  11.7 0.0 copy-start.4
  11.7 0.7 %copy-done.4 = f32[1,2]{1,0:T(1,128)S(1)} copy-done((f32[1,2]{1,0:T(1,128)S(1)}, f32[1,2]{1,0:T(1,128)}, u32[]{:S(2)}) %copy-start.4) | copy-done | bytes 32
  12.3 0.0 copy-start.5
  12.4 0.7 %copy-done.5 = f32[1,2]{1,0:T(1,128)S(1)} copy-done((f32[1,2]{1,0:T(1,128)S(1)}, f32[1,2]{1,0:T(1,128)}, u32[]{:S(2)}) %copy-start.5) | copy-done | bytes 32
  13.0 4.0 %moments.1 = (f32[64,4,128]{2,1,0:T(4,128)S(1)}, f32[2,32,128]{2,1,0:T(8,128)S(1)}) custom-call(s32[16,3]{1,0:T(8,128)S(1)} %copy.13.hop_s, s32[16]{0:T(128)S(1)} %copy-done.3, f32[1,2]{1,0:T(1,128)S(1)} %copy-done.4, f32[1,2]{1,0:T(1,128)S(1)} %copy-done.5, f32[2,16,32,128]{3,2,1,0:T(8,128)S(1)} %all_gather.3.both_ref, ...), custom_call_target="tpu_custom_call" | custom-call | tf_op jit(solution)/shard_map/moments/pallas_call | solution.py:307
  17.0 37.3 %all_to_all.5.mom_ref = f32[64,4,128]{2,1,0:T(4,128)S(1)} all-to-all(f32[64,4,128]{2,1,0:T(4,128)S(1)} %get-tuple-element.11), channel_id=1, replica_groups={{128,256,130,258,132,260,134,262,8,392,10,394,12,396,14,398,144,272,146..., dimensions={0} | all-to-all | bytes 262144 | tf_op jit(solution)/shard_map/all_to_all | solution.py:327
  54.3 0.0 copy-done
  54.3 1.3 %combine.1 = f32[1,2,32,128]{3,2,1,0:T(8,128)} custom-call(f32[64,4,128]{2,1,0:T(4,128)S(1)} %all_to_all.5.mom_ref, f32[1,16,32,128]{3,2,1,0:T(8,128)S(1)} %copy-done, f32[2,32,128]{2,1,0:T(8,128)S(1)} %get-tuple-element.12.img_ref), custom_call_target="tpu_custom_call" | custom-call | tf_op jit(solution)/shard_map/combine/pallas_call | solution.py:328
  (4 shorter events, 0.0 us)
Async XLA Ops:
  3.3 7.7 %collective-permute-start = (f32[264,128]{1,0:T(8,128)S(1)}, f32[264,128]{1,0:T(8,128)S(1)}, u32[]{:S(2)}, u32[]{:S(2)}) collective-permute-start(f32[264,128]{1,0:T(8,128)S(1)} %pad_maximum_fusion), channel_id=1, source_target_pairs={{0,2},{1,3},{2,4},{3,5},{4,6},{5,7},{6,8},{7,9},{8,10},{9,11},{10,... | collective-permute-start | bytes 405512 | tf_op jit(solution)/shard_map/ppermute | solution.py:295
  5.4 1.0 %copy-start.1 = (f32[8,2,64,64]{3,2,1,0:T(8,128)S(1)}, f32[8,2,64,64]{3,2,1,0:T(8,128)}, u32[]{:S(2)}) copy-start(f32[8,2,64,64]{3,2,1,0:T(8,128)} %hop_ref.1) | copy-start | bytes 786436
  6.4 0.9 %copy-start.2 = (f32[4,2,64,64]{3,2,1,0:T(8,128)S(1)}, f32[4,2,64,64]{3,2,1,0:T(8,128)}, u32[]{:S(2)}) copy-start(f32[4,2,64,64]{3,2,1,0:T(8,128)} %pair_ref.1) | copy-start | bytes 393220
  7.4 46.9 %copy-start = (f32[1,16,32,128]{3,2,1,0:T(8,128)S(1)}, f32[1,16,32,128]{3,2,1,0:T(8,128)}, u32[]{:S(2)}) copy-start(f32[1,16,32,128]{3,2,1,0:T(8,128)} %right_ref.1) | copy-start | bytes 786436
  11.0 0.7 %copy-start.3 = (s32[16]{0:T(128)S(1)}, s32[16]{0:T(128)}, u32[]{:S(2)}) copy-start(s32[16]{0:T(128)} %pair_s.1) | copy-start | bytes 196
  11.7 0.7 %copy-start.4 = (f32[1,2]{1,0:T(1,128)S(1)}, f32[1,2]{1,0:T(1,128)}, u32[]{:S(2)}) copy-start(f32[1,2]{1,0:T(1,128)} %shift_s.1) | copy-start | bytes 28
  12.3 0.7 %copy-start.5 = (f32[1,2]{1,0:T(1,128)S(1)}, f32[1,2]{1,0:T(1,128)}, u32[]{:S(2)}) copy-start(f32[1,2]{1,0:T(1,128)} %weight_s.1) | copy-start | bytes 28

commit v2 on v1

v2 whole, which is shorter than its diff:
```python
import jax
import jax.numpy as jnp
from jax import lax
from jax.experimental import pallas as pl
from jax.experimental.pallas import tpu as pltpu
from jax.sharding import PartitionSpec as P

ALL = ("shift", "dom", "eh")
F32 = jnp.float32
BF16 = jnp.bfloat16
SHIFTS, DOMS, EHS = 8, 32, 2
BLK, COLS, LANES = 16, 32, 128
HALF = BLK // 2
WIN = HALF + 6
REACH = HALF + 2
VM = pltpu.CompilerParams(vmem_limit_bytes=24 * 1024 * 1024)


def flat(s, d, e):
    return (s * DOMS + d) * EHS + e


TURNS = {(0, 1): 1, (1, 0): 2, (1, 1): 3, (2, 0): 4, (16, 1): 5, (17, 0): 6, (17, 1): 7}
POINT_AT = [(0, 0)] + list(TURNS)


def halo_pairs():
    pairs = []
    for s in range(SHIFTS):
        for d in range(DOMS):
            for e in range(EHS):
                source = d - 1 + 2 * e
                if 0 <= source < DOMS:
                    turn = TURNS.get((d, e), 0)
                    pairs.append((flat(s ^ turn, source, e), flat(s, d, e)))
    return pairs


def halves(shape):
    lane = lax.broadcasted_iota(jnp.int32, shape, len(shape) - 1)
    return jnp.where(lane < LANES // 2, 1.0, -1.0).astype(F32)


def split3(x):
    a = x.astype(BF16)
    r = x - a.astype(F32)
    b = r.astype(BF16)
    c = (r - b.astype(F32)).astype(BF16)
    return a, b, c


def quad(a, b, c, d):
    return jnp.concatenate(
        [jnp.concatenate([a, b], 1), jnp.concatenate([c, d], 1)], 0
    )


def tables_kernel(hop_ref, pair_ref, hop_out, pair_out):
    def put(out, at, mat):
        out[at] = jnp.concatenate(split3(mat), 1)

    for t in range(8):
        re, im = hop_ref[t, 0], hop_ref[t, 1]
        ret, imt = re.T, im.T
        bwd = quad(re, im, -im, re)
        fwd = quad(ret, imt, -imt, ret)
        put(hop_out, 3 * t, fwd)
        put(hop_out, 3 * t + 1, bwd)
        put(hop_out, 3 * t + 2, fwd + bwd)
    for t in range(4):
        re, im = pair_ref[t, 0], pair_ref[t, 1]
        ret, imt = re.T, im.T
        put(pair_out, 2 * t, quad(ret, imt, imt, -ret))
        put(pair_out, 2 * t + 1, quad(-re, im, im, re))


def product(lhs, tabs):
    rows = lhs.shape[0] // 3
    both = jnp.concatenate([t[:, : 2 * LANES] for t in tabs], 0)
    third = jnp.concatenate([t[:, 2 * LANES :] for t in tabs], 0)
    big = jnp.dot(lhs, both, preferred_element_type=F32)
    small = jnp.dot(lhs[:rows], third, preferred_element_type=F32)
    small = small + big[2 * rows :, :LANES] + big[rows : 2 * rows, LANES:]
    small = small + (big[:rows, LANES:] + big[rows : 2 * rows, :LANES])
    return big[:rows, :LANES] + small


def crossed(block):
    ref, at = block
    zero = jnp.zeros((COLS, LANES), BF16)
    rows = []
    for part in range(3):
        rows += [ref[at, pl.ds((2 * part + 1) * COLS, COLS)], zero]
    return jnp.concatenate(rows, 0)


def crossed_up(block):
    ref, at = block
    zero = jnp.zeros((COLS, LANES), BF16)
    rows = []
    for part in range(3):
        rows += [zero, ref[at, pl.ds(2 * part * COLS, COLS)]]
    return jnp.concatenate(rows, 0)


def image(blocks, hop_t, pair_t, kinds):
    back2, back1, here, on1, on2, pair = kinds
    lhs = [ref[at] for ref, at in blocks]
    lhs += [crossed(blocks[2]), crossed_up(blocks[2])]
    tabs = [hop_t[3 * back2 + 1], hop_t[3 * back1 + 1], hop_t[3 * here + 2]]
    tabs += [hop_t[3 * on1], hop_t[3 * on2], pair_t[2 * pair], pair_t[2 * pair + 1]]
    return product(jnp.concatenate(lhs, 1), tabs)


def forward_image(blocks, hop_t, pair_t, kinds):
    here, on1, on2, pair = kinds
    lhs = [ref[at] for ref, at in blocks] + [-crossed(blocks[0])]
    tabs = [hop_t[3 * here], hop_t[3 * on1], hop_t[3 * on2], pair_t[2 * pair]]
    return product(jnp.concatenate(lhs, 1), tabs)


def swap(x):
    return pltpu.roll(x, LANES // 2, 1)


def add_pairs(re, im, n, a, b, b_swapped):
    re[n] = a * b if re[n] is None else re[n] + a * b
    im[n] = a * b_swapped if im[n] is None else im[n] + a * b_swapped


def fetch_kernel(
    hop_s, pair_s, shift_ref, weight_ref, hop_ref, pair_ref,
    facts_ref, hop_v, pair_v,
    hop_k, pair_k, shift_v, weight_v, sem,
):
    copies = [
        pltpu.make_async_copy(source, to, sem.at[n])
        for n, (source, to) in enumerate(
            (
                (hop_s, hop_k),
                (pair_s, pair_k),
                (shift_ref, shift_v),
                (weight_ref, weight_v),
                (hop_ref, hop_v),
                (pair_ref, pair_v),
            )
        )
    ]
    for c in copies:
        c.start()
    facts_ref[...] = jnp.zeros_like(facts_ref)
    facts_ref[6:7] = jnp.ones((1, LANES), F32)
    for c in copies:
        c.wait()
    facts_ref[0:3, :BLK] = hop_k[...].astype(F32)
    facts_ref[3:4, :BLK] = pair_k[...].astype(F32)
    facts_ref[4:5, :2] = shift_v[...]
    facts_ref[5:6, :2] = weight_v[...]


def parts_of(elec, hole, sign):
    return jnp.concatenate(split3(jnp.concatenate([elec, hole * sign], 0)), 0)


def inner_kernel(
    win_ref, own_ref, hop_t, pair_t,
    us_ref, g_ref, gs_ref, acc_ref,
    own_s, kind_s, sem,
):
    facts = pltpu.make_async_copy(own_ref.at[pl.ds(8 * COLS, 8)], own_s, sem)
    facts.start()
    low = lax.axis_index("eh") == 0
    sign = halves((1, LANES))
    for a in range(10):
        us_ref[a] = parts_of(win_ref[0, a], win_ref[1, a], sign)
    facts.wait()
    for a in range(8):
        for c in range(4):
            kind_s[a, c] = jnp.where(low, own_s[c, a], own_s[c, 6 + a]).astype(jnp.int32)
    re, im = [None] * 4, [None] * 4
    for k in range(6):
        kinds = [kind_s[k, 2], kind_s[k + 1, 1]] + [kind_s[k + 2, c] for c in range(4)]
        g = image([(us_ref, k + n) for n in range(5)], hop_t, pair_t, kinds)
        g_ref[k] = g
        gs_ref[k] = jnp.concatenate(split3(g), 0)
        u = jnp.concatenate([win_ref[0, k + 2], win_ref[1, k + 2] * sign], 0)
        add_pairs(re, im, 0, u, u, swap(u))
        add_pairs(re, im, 1, u, g, swap(g))
        add_pairs(re, im, 2, g, g, swap(g))
    for k in range(4):
        kinds = [kind_s[k + 2, c] for c in range(4)]
        y = forward_image([(gs_ref, k + n) for n in range(3)], hop_t, pair_t, kinds)
        add_pairs(re, im, 3, g_ref[k], y, swap(y))
    for n in range(4):
        acc_ref[2 * n] = re[n]
        acc_ref[2 * n + 1] = im[n]


def outer_side(
    low, win_ref, both_ref, recv_ref, hop_t, pair_t, us_in, g_in, gs_in, acc_ref,
    total_ref, us_new, g_ref, gs_new, own_s, recv_s, kind_s, waits, valid,
):
    off = 2 if low else 0
    base = 0 if low else HALF
    sign = halves((1, LANES))
    edge = [0, 1, 12, 13] if low else [10, 11, 12, 13]
    for n, j in enumerate(edge):
        i = base + j - 2
        if 0 <= i < BLK:
            elec, hole = both_ref[0, i], both_ref[1, i]
        else:
            at = i % 4
            elec = recv_ref[pl.ds(at * COLS, COLS)]
            hole = recv_ref[pl.ds((4 + at) * COLS, COLS)]
        us_new[n] = parts_of(elec, hole, sign)
    for k in range(6):
        g_ref[off + k] = g_in[k]
    for c in waits:
        c.wait()
    for j in range(WIN - 2):
        i = base + j - 2
        for c in range(4):
            fact = own_s[c, i] if 0 <= i < BLK else recv_s[c, i % BLK]
            kind_s[j, c] = fact.astype(jnp.int32)

    def us(j):
        return (us_new, edge.index(j)) if j in edge else (us_in, j - off)

    images = [0, 1, 8, 9] if low else [6, 7, 8, 9]

    def gs(m):
        return (gs_new, images.index(m)) if m in images else (gs_in, m - off)

    re = [acc_ref[2 * n] for n in range(4)]
    im = [acc_ref[2 * n + 1] for n in range(4)]
    for n, m in enumerate(images):
        j = m + 2
        kinds = [kind_s[j - 2, 2], kind_s[j - 1, 1]] + [kind_s[j, c] for c in range(4)]
        g = image([us(j - 2 + k) for k in range(5)], hop_t, pair_t, kinds)
        if base + m >= BLK:
            g = jnp.where(valid(), g, 0.0)
        g_ref[m] = g
        gs_new[n] = jnp.concatenate(split3(g), 0)
        if m < HALF:
            i = base + m
            u = jnp.concatenate([both_ref[0, i], both_ref[1, i] * sign], 0)
            add_pairs(re, im, 0, u, u, swap(u))
            add_pairs(re, im, 1, u, g, swap(g))
            add_pairs(re, im, 2, g, g, swap(g))
    for m in [0, 1, 6, 7] if low else [4, 5, 6, 7]:
        kinds = [kind_s[m + 2, c] for c in range(4)]
        y = forward_image([gs(m + k) for k in range(3)], hop_t, pair_t, kinds)
        add_pairs(re, im, 3, g_ref[m], y, swap(y))
    for n in range(4):
        s = 1.0 if n in (0, 2) else -1.0
        w = 2.0 if n == 3 else 1.0
        total_ref[2 * n] = w * sign * (re[n][:COLS] + s * re[n][COLS:])
        total_ref[2 * n + 1] = w * (im[n][:COLS] - s * im[n][COLS:])


def outer_kernel(
    win_ref, both_ref, own_ref, recv_ref, hop_t, pair_t, us_in, g_in, gs_in, acc_ref,
    send_ref, img_ref,
    total_ref, us_new, g_ref, gs_new, own_s, recv_s, kind_s, sem,
):
    copies = [
        pltpu.make_async_copy(own_ref.at[pl.ds(8 * COLS, 8)], own_s, sem.at[0]),
        pltpu.make_async_copy(recv_ref.at[pl.ds(8 * COLS, 8)], recv_s, sem.at[1]),
    ]
    for c in copies:
        c.start()
    point, eh = lax.axis_index("shift"), lax.axis_index("eh")

    def valid():
        return recv_s[6, 0] > 0.5

    for side in range(2):

        @pl.when(eh == side)
        def _(side=side):
            outer_side(
                side == 0, win_ref, both_ref, recv_ref, hop_t, pair_t, us_in, g_in, gs_in, acc_ref,
                total_ref, us_new, g_ref, gs_new, own_s, recv_s, kind_s, copies, valid,
            )

    low = eh == 0
    sign = halves((1, LANES))
    ones = jnp.ones((8, LANES), F32)
    for k in range(2):
        total = lax.dot_general(
            ones, total_ref[4 * k : 4 * k + 4].reshape(4 * COLS, LANES), (((1,), (1,)), ((), ())),
            precision=lax.Precision.HIGHEST, preferred_element_type=F32,
        )
        send_ref[k : k + 1] = total[:1]
    facts = jnp.where(valid(), recv_ref[8 * COLS :], own_ref[8 * COLS :])
    send_ref[2:3] = facts[4:5] + pltpu.roll(facts[5:6], 2, 1)
    send_ref[3:8] = jnp.zeros((5, LANES), F32)
    first = 2 * jnp.bitwise_and(point, 3)
    for k in range(2):
        g = g_ref[first + k]
        elec, hole = g[:COLS], -sign * g[COLS:]
        img_ref[k] = jnp.where(low, elec, hole)
        send_ref[(1 + 4 * k) * 8 : (5 + 4 * k) * 8] = jnp.where(low, hole, elec)


def cmul(a, b):
    return a[0] * b[0] - a[1] * b[1], a[0] * b[1] + a[1] * b[0]


def cadd(a, b):
    return a[0] + b[0], a[1] + b[1]


def cdiv(a, b):
    denom = jnp.maximum(b[0] * b[0] + b[1] * b[1], 1.0)
    return (a[0] * b[0] + a[1] * b[1]) / denom, (a[1] * b[0] - a[0] * b[1]) / denom


def combine_kernel(mom_ref, right_ref, img_ref, sent_ref, out_ref):
    total = jnp.sum(mom_ref[...], axis=0)
    pts = jnp.concatenate([mom_ref[d, 2 + e : 3 + e] for d, e in POINT_AT], 0)

    def moment(n):
        row = total[n // 2 : n // 2 + 1]
        at = (n % 2) * 64
        return tuple(
            jnp.broadcast_to(row[:, at + k * COLS : at + (k + 1) * COLS], (SHIFTS, COLS))
            for k in range(2)
        )

    def param(n):
        return tuple(
            jnp.broadcast_to(pts[:, n + k : n + k + 1], (SHIFTS, COLS)) for k in range(2)
        )

    m0, m1, m2, m3 = (moment(n) for n in range(4))
    z, w = param(0), param(2)

    def minus(a, b):
        return a[0] - b[0], a[1] - b[1]

    def twice(a):
        return 2.0 * a[0], 2.0 * a[1]

    a0 = cdiv(m0, minus(cmul(z, m0), m1))
    az = cmul(a0, z)
    s = (1.0 - az[0], -az[1])
    s2, sa, aa = cmul(s, s), cmul(s, a0), cmul(a0, a0)
    rho = cadd(cadd(cmul(s2, m0), twice(cmul(sa, m1))), cmul(aa, m2))
    c = cadd(s, cdiv(rho, m0))
    cc, ca = cmul(c, c), cmul(c, a0)
    pp = cadd(cadd(cmul(cc, m0), twice(cmul(ca, m1))), cmul(aa, m2))
    php = cadd(cadd(cmul(cc, m1), twice(cmul(ca, m2))), cmul(aa, m3))
    a1 = cdiv(rho, minus(cmul(z, pp), php))
    c0 = cmul(w, cadd(a0, cmul(a1, c)))
    c1 = cmul(w, cmul(a1, a0))
    rows = [jnp.sum(x, axis=0, keepdims=True) for x in (*c0, *c1)]
    stack = jnp.concatenate(rows + [jnp.zeros((4, COLS), F32)], 0)
    stack = jnp.concatenate([stack, jnp.zeros((8, LANES - COLS), F32)], 1)
    cols = stack.T[:COLS]
    sign = -halves((1, LANES))
    point = lax.axis_index("shift")
    holder = (point >= SHIFTS // 2).astype(jnp.int32)
    mine = lax.axis_index("eh") == holder
    for k in range(2):
        b = right_ref[0, 2 * point + k]
        g = jnp.where(mine, img_ref[k], sent_ref[holder, (1 + 4 * k) * 8 : (5 + 4 * k) * 8])
        out = cols[:, 0:1] * b + cols[:, 1:2] * (pltpu.roll(b, LANES // 2, 1) * sign)
        out = out + cols[:, 2:3] * g + cols[:, 3:4] * (pltpu.roll(g, LANES // 2, 1) * sign)
        out_ref[0, k] = out


def body(right_side, shifts, quad_weights, hop_table, pair_table, hop_type, pair_type):
    vmem = pl.BlockSpec(memory_space=pltpu.VMEM)
    low = lax.axis_index("eh") == 0
    inputs = (hop_type.T, pair_type[None], shifts, quad_weights, hop_table, pair_table)
    facts, hops, pairs = pl.pallas_call(
        fetch_kernel,
        out_shape=[
            jax.ShapeDtypeStruct((8, LANES), F32),
            jax.ShapeDtypeStruct(hop_table.shape, F32),
            jax.ShapeDtypeStruct(pair_table.shape, F32),
        ],
        in_specs=[pl.BlockSpec(memory_space=pltpu.HBM)] * 6,
        out_specs=[vmem] * 3,
        scratch_shapes=[
            pltpu.VMEM((3, BLK), jnp.int32),
            pltpu.VMEM((1, BLK), jnp.int32),
            pltpu.VMEM((1, 2), F32),
            pltpu.VMEM((1, 2), F32),
            pltpu.SemaphoreType.DMA((6,)),
        ],
        compiler_params=VM,
        name="fetch",
    )(*(pltpu.with_memory_space_constraint(x, pltpu.HBM) for x in inputs))
    both = lax.all_gather(right_side[0], "eh")
    edge = lax.dynamic_slice_in_dim(both, jnp.where(low, BLK - 4, 0), 4, 1)
    own = jnp.concatenate([edge.reshape(8 * COLS, LANES), facts], 0)
    recv = lax.ppermute(own, ALL, halo_pairs())
    hop_t, pair_t = pl.pallas_call(
        tables_kernel,
        out_shape=[
            jax.ShapeDtypeStruct((24, LANES, 3 * LANES), BF16),
            jax.ShapeDtypeStruct((8, LANES, 3 * LANES), BF16),
        ],
        in_specs=[vmem] * 2,
        out_specs=[vmem] * 2,
        compiler_params=VM,
        name="tables",
    )(hops, pairs)
    win = lax.dynamic_slice_in_dim(both, jnp.where(low, 0, 6), 10, 1)
    us, g, gs, acc = pl.pallas_call(
        inner_kernel,
        out_shape=[
            jax.ShapeDtypeStruct((10, 6 * COLS, LANES), BF16),
            jax.ShapeDtypeStruct((6, 2 * COLS, LANES), F32),
            jax.ShapeDtypeStruct((6, 6 * COLS, LANES), BF16),
            jax.ShapeDtypeStruct((8, 2 * COLS, LANES), F32),
        ],
        in_specs=[vmem] * 4,
        out_specs=[vmem] * 4,
        scratch_shapes=[
            pltpu.SMEM((8, LANES), F32),
            pltpu.SMEM((8, 4), jnp.int32),
            pltpu.SemaphoreType.DMA,
        ],
        compiler_params=VM,
        name="inner",
    )(win, own, hop_t, pair_t)
    send, img = pl.pallas_call(
        outer_kernel,
        out_shape=[
            jax.ShapeDtypeStruct((72, LANES), F32),
            jax.ShapeDtypeStruct((2, COLS, LANES), F32),
        ],
        in_specs=[vmem] * 10,
        out_specs=[vmem] * 2,
        scratch_shapes=[
            pltpu.VMEM((8, COLS, LANES), F32),
            pltpu.VMEM((4, 6 * COLS, LANES), BF16),
            pltpu.VMEM((REACH, 2 * COLS, LANES), F32),
            pltpu.VMEM((4, 6 * COLS, LANES), BF16),
            pltpu.SMEM((8, LANES), F32),
            pltpu.SMEM((8, LANES), F32),
            pltpu.SMEM((WIN, 4), jnp.int32),
            pltpu.SemaphoreType.DMA((2,)),
        ],
        compiler_params=VM,
        name="outer",
    )(win, both, own, recv, hop_t, pair_t, us, g, gs, acc)
    sent = lax.all_gather(send, "eh")
    mom = jnp.concatenate([sent[0, :2] + sent[1, :2], sent[:, 2]], 0)
    mom = jnp.broadcast_to(mom[None], (DOMS, 4, LANES))
    parts = lax.all_to_all(mom, "dom", 0, 0)
    return pl.pallas_call(
        combine_kernel,
        out_shape=jax.ShapeDtypeStruct((1, 2, COLS, LANES), F32),
        in_specs=[vmem] * 4,
        out_specs=vmem,
        compiler_params=VM,
        name="combine",
    )(parts, right_side, img, sent)


def solution(mesh):
    placed = (
        P("eh", "dom", None, None),
        P("shift", None),
        P("shift", None),
        P(),
        P(),
        P("dom", None),
        P("dom"),
    )
    return jax.shard_map(
        body,
        mesh=mesh,
        in_specs=placed,
        out_specs=P("eh", ("dom", "shift"), None, None),
        check_vma=False,
    )
```

time: 56.7 us -> 48.2 us (0.85); the launches traced: 55.6 us -> 48.1 us
  local copies, waits for them, and re-layouts: 4.91 us -> 0.07 us
  blocking collectives: 39.7 us -> 36.1 us
  waiting for transfers between devices: 2.74 us -> 0.01 us
  starting transfers between devices: 1.29 us -> 4.01 us
  Pallas kernels: 6.23 us -> 7.82 us
  other arithmetic: 0.72 us -> 0.03 us
    all_to_all x1, blocking collectives: 37.3 us -> 30.8 us  [body(): parts = lax.all_to_all(mom, 'dom', 0, 0)]
    unnamed x13 -> x2, local copies, waits for them, and re-layouts: 4.72 us -> 0.01 us
    all_gather x0 -> x1, blocking collectives: none -> 2.92 us  [body(): sent = lax.all_gather(send, 'eh')]
    ppermute x1, waiting for transfers between devices: 2.74 us -> 0.01 us  [body(): recv = lax.ppermute(own, ALL, halo_pairs())]
    ppermute x1, starting transfers between devices: 1.29 us -> 4.01 us  [body(): recv = lax.ppermute(own, ALL, halo_pairs())]
    pallas_call x1 -> x3, Pallas kernels: 4.01 us -> 5.59 us  [the longest x1 2.22 us: body(): pl.pallas_call(outer_kernel, out_shape=[jax.ShapeDtypeStruct((72, LANES),...]
    convert_element_type x1 -> x0, other arithmetic: 0.71 us -> none  [body(): jnp.concatenate([hop_type, pair_type[:, None]], 1).astype(F32)]
  transfers between devices with their start and end apart: 1 -> 1, of which waited for: 1 -> 0; matrix products, arithmetic and copies ran while one was open for 1% -> 0% of each run, Pallas kernels for 2% -> 6%
where the time goes in v2:
time: 48.2 us; the launch traced here: 48.1 us
  blocking collectives  36.1 us (75%)
  Pallas kernels  7.82 us (16%)
  starting transfers between devices  4.01 us (8%)
    all_to_all x1, blocking collectives, body(): parts = lax.all_to_all(mom, 'dom', 0, 0)  30.8 us
    ppermute x1, starting transfers between devices, body(): recv = lax.ppermute(own, ALL, halo_pairs())  4.01 us
    all_gather x1, blocking collectives, body(): sent = lax.all_gather(send, 'eh')  2.92 us
    all_gather x1, blocking collectives, body(): both = lax.all_gather(right_side[0], 'eh')  2.38 us
    pallas_call x1, Pallas kernels, body(): pl.pallas_call(outer_kernel, out_shape=[jax.ShapeDtypeStruct((72, LANES),...  2.22 us
    pallas_call x1, Pallas kernels, body(): pl.pallas_call(inner_kernel, out_shape=[jax.ShapeDtypeStruct((10, 6 * COL...  2.13 us
    pallas_call x1, Pallas kernels, body(): pl.pallas_call(combine_kernel, out_shape=jax.ShapeDtypeStruct((1, 2, COLS...  1.33 us
    pallas_call x1, Pallas kernels, body(): pl.pallas_call(fetch_kernel, out_shape=[jax.ShapeDtypeStruct((8, LANES),...  1.23 us
  transfers between devices with their start and end apart: 1, of which 0 were waited for; matrix products, arithmetic and copies ran while one was open for 0% of the time, Pallas kernels for 6%

profile of v2, /device:TPU:24, one launch (start us, length us, event | category | flops | bytes accessed | tf_op | source)
XLA Modules:
  0.0 48.1 jit_solution(2123954884416687850)
XLA Ops:
  0.0 2.4 %all_gather.9.both_ref = f32[2,16,32,128]{3,2,1,0:T(8,128)S(1)} all-gather(f32[1,16,32,128]{3,2,1,0:T(8,128)} %right_ref.1), channel_id=1, replica_groups=mesh['shift'=8,'dom'=32,'eh'=2] {'eh'}, dimensions={0}, use_global_device_ids=true | all-gather | bytes 786432 | tf_op jit(solution)/shard_map/all_gather | solution.py:396
  2.4 1.2 %fetch.1 = (f32[8,128]{1,0:T(8,128)S(1)}, f32[8,2,64,64]{3,2,1,0:T(8,128)S(1)}, f32[4,2,64,64]{3,2,1,0:T(8,128)S(1)}) custom-call(s32[3,16]{1,0:T(4,128)} %bitcast.12, s32[1,16]{1,0:T(1,128)} %bitcast.13, f32[1,2]{1,0:T(1,128)} %shift_ref.1, f32[1,2]{1,0:T(1,128)} %weight_ref.1, f32[8,2,64,64]{3,2,1,0:T(8,128)} %hop_ref.1, f32[4,2,64,64]{3,2,1,0:T(8,128)} %pair_ref.1), custom_call_target="tpu_custom_call" | custom-call | tf_op jit(solution)/shard_map/fetch/pallas_call | solution.py:377
  3.7 4.0 %collective-permute-start = (f32[264,128]{1,0:T(8,128)S(1)}, f32[264,128]{1,0:T(8,128)S(1)}, u32[]{:S(2)}, u32[]{:S(2)}) collective-permute-start(f32[264,128]{1,0:T(8,128)S(1)} %pad_maximum_fusion.own_ref), channel_id=1, source_target_pairs={{67,1},{128,2},{197,3},{258,4},{7,5},{4,6},{9,7},{6,8},{11,9},{8,1... | collective-permute-start | bytes 405512 | tf_op jit(solution)/shard_map/ppermute | solution.py:399
  7.7 0.9 %tables.1 = (bf16[24,128,384]{2,1,0:T(8,128)(2,1)S(1)}, bf16[8,128,384]{2,1,0:T(8,128)(2,1)S(1)}) custom-call(f32[8,2,64,64]{3,2,1,0:T(8,128)S(1)} %get-tuple-element.17.hop_ref, f32[4,2,64,64]{3,2,1,0:T(8,128)S(1)} %get-tuple-element.18.pair_ref), custom_call_target="tpu_custom_call" | custom-call | tf_op jit(solution)/shard_map/tables/pallas_call | solution.py:400
  8.6 2.1 %inner.1 = (bf16[10,192,128]{2,1,0:T(8,128)(2,1)S(1)}, f32[6,64,128]{2,1,0:T(8,128)S(1)}, bf16[6,192,128]{2,1,0:T(8,128)(2,1)S(1)}, f32[8,64,128]{2,1,0:T(8,128)S(1)}) custom-call(f32[2,10,32,128]{3,2,1,0:T(8,128)S(1)} %constant_dynamic-slice_fusion.1.win_ref, f32[264,128]{1,0:T(8,128)S(1)} %pad_maximum_fusion.own_ref, ...), custom_call_target="tpu_custom_call" | custom-call | tf_op jit(solution)/shard_map/inner/pallas_call | solution.py:412
  10.8 0.0 collective-permute-done.recv_ref
  10.8 0.0 copy-start
  10.8 2.2 %outer.1 = (f32[72,128]{1,0:T(8,128)S(1)}, f32[2,32,128]{2,1,0:T(8,128)S(1)}) custom-call(f32[2,10,32,128]{3,2,1,0:T(8,128)S(1)} %constant_dynamic-slice_fusion.1.win_ref, f32[2,16,32,128]{3,2,1,0:T(8,128)S(1)} %all_gather.9.both_ref, f32[264,128]{1,0:T(8,128)S(1)} %pad_maximum_fusion.own_ref, f32[264,128]{1,0:T(8,128)S(1)} %collective-permute-done.recv_ref, ...), custom_call_target="tpu_custom_call" | custom-call | tf_op jit(solution)/shard_map/outer/pallas_call | solution.py:430
  13.0 2.9 %all-gather = f32[144,128]{1,0:T(8,128)S(1)} all-gather(f32[72,128]{1,0:T(8,128)S(1)} %get-tuple-element.25), channel_id=2, replica_groups=mesh['shift'=8,'dom'=32,'eh'=2] {'eh'}, dimensions={0}, use_global_device_ids=true | all-gather | bytes 110592 | tf_op jit(solution)/shard_map/all_gather | solution.py:451
  16.0 30.8 %all_to_all.5.mom_ref = f32[32,4,128]{2,1,0:T(4,128)S(1)} all-to-all(f32[32,4,128]{2,1,0:T(4,128)S(1)} %broadcast_in_dim.10), channel_id=1, replica_groups=mesh['shift'=8,'dom'=32,'eh'=2] {'dom'}, dimensions={0} | all-to-all | bytes 131072 | tf_op jit(solution)/shard_map/all_to_all | solution.py:454
  46.7 0.0 copy-done
  46.7 1.3 %combine.1 = f32[1,2,32,128]{3,2,1,0:T(8,128)} custom-call(f32[32,4,128]{2,1,0:T(4,128)S(1)} %all_to_all.5.mom_ref, f32[1,16,32,128]{3,2,1,0:T(8,128)S(1)} %copy-done, f32[2,32,128]{2,1,0:T(8,128)S(1)} %get-tuple-element.26.img_ref, f32[2,72,128]{2,1,0:T(8,128)S(1)} %bitcast.9), custom_call_target="tpu_custom_call" | custom-call | tf_op jit(solution)/shard_map/combine/pallas_call | solution.py:455
  (7 shorter events, 0.1 us)
Async XLA Ops:
  3.7 7.1 %collective-permute-start = (f32[264,128]{1,0:T(8,128)S(1)}, f32[264,128]{1,0:T(8,128)S(1)}, u32[]{:S(2)}, u32[]{:S(2)}) collective-permute-start(f32[264,128]{1,0:T(8,128)S(1)} %pad_maximum_fusion.own_ref), channel_id=1, source_target_pairs={{67,1},{128,2},{197,3},{258,4},{7,5},{4,6},{9,7},{6,8},{11,9},{8,1... | collective-permute-start | bytes 405512 | tf_op jit(solution)/shard_map/ppermute | solution.py:399
  10.8 36.0 %copy-start = (f32[1,16,32,128]{3,2,1,0:T(8,128)S(1)}, f32[1,16,32,128]{3,2,1,0:T(8,128)}, u32[]{:S(2)}) copy-start(f32[1,16,32,128]{3,2,1,0:T(8,128)} %right_ref.1) | copy-start | bytes 786436

commit v3 on v2

--- a/solution.py
+++ b/solution.py
@@ -10,9 +10,11 @@
 BF16 = jnp.bfloat16
 SHIFTS, DOMS, EHS = 8, 32, 2
 BLK, COLS, LANES = 16, 32, 128
-HALF = BLK // 2
-WIN = HALF + 6
-REACH = HALF + 2
+EDGE = 3
+INNER = 11
+REACH = 10
+SPLIT = 7
+ROWS = 2 * EDGE * COLS
 VM = pltpu.CompilerParams(vmem_limit_bytes=24 * 1024 * 1024)
 
 
@@ -167,27 +169,29 @@
     us_ref, g_ref, gs_ref, acc_ref,
     own_s, kind_s, sem,
 ):
-    facts = pltpu.make_async_copy(own_ref.at[pl.ds(8 * COLS, 8)], own_s, sem)
+    facts = pltpu.make_async_copy(own_ref.at[pl.ds(ROWS, 8)], own_s, sem)
     facts.start()
     low = lax.axis_index("eh") == 0
     sign = halves((1, LANES))
-    for a in range(10):
+    for a in range(INNER):
         us_ref[a] = parts_of(win_ref[0, a], win_ref[1, a], sign)
     facts.wait()
-    for a in range(8):
+    for a in range(INNER - 2):
         for c in range(4):
-            kind_s[a, c] = jnp.where(low, own_s[c, a], own_s[c, 6 + a]).astype(jnp.int32)
+            kind_s[a, c] = jnp.where(low, own_s[c, a], own_s[c, BLK - INNER + a]).astype(jnp.int32)
     re, im = [None] * 4, [None] * 4
-    for k in range(6):
+    for k in range(INNER - 4):
         kinds = [kind_s[k, 2], kind_s[k + 1, 1]] + [kind_s[k + 2, c] for c in range(4)]
         g = image([(us_ref, k + n) for n in range(5)], hop_t, pair_t, kinds)
         g_ref[k] = g
         gs_ref[k] = jnp.concatenate(split3(g), 0)
         u = jnp.concatenate([win_ref[0, k + 2], win_ref[1, k + 2] * sign], 0)
+        if k + 2 >= SPLIT:
+            u, g = jnp.where(low, 0.0, u), jnp.where(low, 0.0, g)
         add_pairs(re, im, 0, u, u, swap(u))
         add_pairs(re, im, 1, u, g, swap(g))
         add_pairs(re, im, 2, g, g, swap(g))
-    for k in range(4):
+    for k in range(INNER - 6):
         kinds = [kind_s[k + 2, c] for c in range(4)]
         y = forward_image([(gs_ref, k + n) for n in range(3)], hop_t, pair_t, kinds)
         add_pairs(re, im, 3, g_ref[k], y, swap(y))
@@ -197,105 +201,100 @@
 
 
 def outer_side(
-    low, win_ref, both_ref, recv_ref, hop_t, pair_t, us_in, g_in, gs_in, acc_ref,
-    total_ref, us_new, g_ref, gs_new, own_s, recv_s, kind_s, waits, valid,
+    low, win_ref, recv_ref, hop_t, pair_t, us_in, g_in, gs_in, acc_ref,
+    us_new, g_ref, gs_new, own, recv, valid,
 ):
-    off = 2 if low else 0
-    base = 0 if low else HALF
+    start = 0 if low else BLK - INNER
+    first = -1 if low else SPLIT
     sign = halves((1, LANES))
-    edge = [0, 1, 12, 13] if low else [10, 11, 12, 13]
-    for n, j in enumerate(edge):
-        i = base + j - 2
-        if 0 <= i < BLK:
-            elec, hole = both_ref[0, i], both_ref[1, i]
-        else:
-            at = i % 4
-            elec = recv_ref[pl.ds(at * COLS, COLS)]
-            hole = recv_ref[pl.ds((4 + at) * COLS, COLS)]
+    edge = [-3, -2, -1] if low else [16, 17, 18]
+    for n in range(EDGE):
+        elec = recv_ref[pl.ds(n * COLS, COLS)]
+        hole = recv_ref[pl.ds((EDGE + n) * COLS, COLS)]
         us_new[n] = parts_of(elec, hole, sign)
-    for k in range(6):
-        g_ref[off + k] = g_in[k]
-    for c in waits:
-        c.wait()
-    for j in range(WIN - 2):
-        i = base + j - 2
-        for c in range(4):
-            fact = own_s[c, i] if 0 <= i < BLK else recv_s[c, i % BLK]
-            kind_s[j, c] = fact.astype(jnp.int32)
-
-    def us(j):
-        return (us_new, edge.index(j)) if j in edge else (us_in, j - off)
-
-    images = [0, 1, 8, 9] if low else [6, 7, 8, 9]
-
-    def gs(m):
-        return (gs_new, images.index(m)) if m in images else (gs_in, m - off)
+    for k in range(INNER - 4):
+        g_ref[start + 2 + k - first] = g_in[k]
+    images = [-1, 0, 1] if low else [14, 15, 16]
+    kinds_of = {}
+    for i in range(-3, 2) if low else range(12, 17):
+        kinds_of[i] = (own if 0 <= i < BLK else recv)[0, i % BLK]
+
+    def kind(i, c):
+        return jnp.bitwise_and(lax.shift_right_logical(kinds_of[i], 3 * c), 7)
+
+    def us(i):
+        return (us_new, edge.index(i)) if i in edge else (us_in, i - start)
+
+    def gs(i):
+        return (gs_new, images.index(i)) if i in images else (gs_in, i - start - 2)
 
     re = [acc_ref[2 * n] for n in range(4)]
     im = [acc_ref[2 * n + 1] for n in range(4)]
-    for n, m in enumerate(images):
-        j = m + 2
-        kinds = [kind_s[j - 2, 2], kind_s[j - 1, 1]] + [kind_s[j, c] for c in range(4)]
-        g = image([us(j - 2 + k) for k in range(5)], hop_t, pair_t, kinds)
-        if base + m >= BLK:
-            g = jnp.where(valid(), g, 0.0)
-        g_ref[m] = g
+    for n, i in enumerate(images):
+        kinds = [kind(i - 2, 2), kind(i - 1, 1)] + [kind(i, c) for c in range(4)]
+        g = image([us(i - 2 + k) for k in range(5)], hop_t, pair_t, kinds)
+        own = 0 <= i < BLK
+        if not own:
+            g = jnp.where(valid, g, 0.0)
+        g_ref[i - first] = g
         gs_new[n] = jnp.concatenate(split3(g), 0)
-        if m < HALF:
-            i = base + m
-            u = jnp.concatenate([both_ref[0, i], both_ref[1, i] * sign], 0)
+        if own:
+            u = jnp.concatenate([win_ref[0, i - start], win_ref[1, i - start] * sign], 0)
             add_pairs(re, im, 0, u, u, swap(u))
             add_pairs(re, im, 1, u, g, swap(g))
             add_pairs(re, im, 2, g, g, swap(g))
-    for m in [0, 1, 6, 7] if low else [4, 5, 6, 7]:
-        kinds = [kind_s[m + 2, c] for c in range(4)]
-        y = forward_image([gs(m + k) for k in range(3)], hop_t, pair_t, kinds)
-        add_pairs(re, im, 3, g_ref[m], y, swap(y))
+    for i in [0, 1] if low else [12, 13, 14]:
+        kinds = [kind(i, c) for c in range(4)]
+        y = forward_image([gs(i + k) for k in range(3)], hop_t, pair_t, kinds)
+        add_pairs(re, im, 3, g_ref[i - first], y, swap(y))
+    if low:
+        ref, at = gs(1)
+        i, y = -1, product(ref[at], [hop_t[3 * kind(-1, 2)]])
+    else:
+        i = BLK - 1
+        lhs = [ref[at] for ref, at in (gs(i), gs(i + 1))] + [-crossed(gs(i))]
+        tabs = [hop_t[3 * kind(i, 0)], hop_t[3 * kind(i, 1)], pair_t[2 * kind(i, 3)]]
+        y = product(jnp.concatenate(lhs, 1), tabs)
+    add_pairs(re, im, 3, g_ref[i - first], y, swap(y))
+    rows = []
     for n in range(4):
         s = 1.0 if n in (0, 2) else -1.0
         w = 2.0 if n == 3 else 1.0
-        total_ref[2 * n] = w * sign * (re[n][:COLS] + s * re[n][COLS:])
-        total_ref[2 * n + 1] = w * (im[n][:COLS] - s * im[n][COLS:])
+        rows.append(w * sign * (re[n][:COLS] + s * re[n][COLS:]))
+        rows.append(w * (im[n][:COLS] - s * im[n][COLS:]))
+    return rows
+
+
+def kinds_row(facts):
+    row = facts[0:1] + 8.0 * facts[1:2] + 64.0 * facts[2:3] + 512.0 * facts[3:4]
+    return row.astype(jnp.int32)
 
 
 def outer_kernel(
-    win_ref, both_ref, own_ref, recv_ref, hop_t, pair_t, us_in, g_in, gs_in, acc_ref,
+    win_ref, own_ref, recv_ref, hop_t, pair_t, us_in, g_in, gs_in, acc_ref,
     send_ref, img_ref,
-    total_ref, us_new, g_ref, gs_new, own_s, recv_s, kind_s, sem,
+    us_new, g_ref, gs_new,
 ):
-    copies = [
-        pltpu.make_async_copy(own_ref.at[pl.ds(8 * COLS, 8)], own_s, sem.at[0]),
-        pltpu.make_async_copy(recv_ref.at[pl.ds(8 * COLS, 8)], recv_s, sem.at[1]),
-    ]
-    for c in copies:
-        c.start()
-    point, eh = lax.axis_index("shift"), lax.axis_index("eh")
-
-    def valid():
-        return recv_s[6, 0] > 0.5
-
+    point, eh, dom = (lax.axis_index(x) for x in ("shift", "eh", "dom"))
+    own, recv = kinds_row(own_ref[ROWS:]), kinds_row(recv_ref[ROWS:])
     for side in range(2):
 
         @pl.when(eh == side)
         def _(side=side):
-            outer_side(
-                side == 0, win_ref, both_ref, recv_ref, hop_t, pair_t, us_in, g_in, gs_in, acc_ref,
-                total_ref, us_new, g_ref, gs_new, own_s, recv_s, kind_s, copies, valid,
+            rows = outer_side(
+                side == 0, win_ref, recv_ref, hop_t, pair_t, us_in, g_in, gs_in, acc_ref,
+                us_new, g_ref, gs_new, own, recv, dom > 0 if side == 0 else dom < DOMS - 1,
             )
+            for k in range(2):
+                total = jnp.concatenate(rows[4 * k : 4 * k + 4], 0).T
+                send_ref[k : k + 1] = jnp.sum(total, axis=0, keepdims=True)
 
     low = eh == 0
     sign = halves((1, LANES))
-    ones = jnp.ones((8, LANES), F32)
-    for k in range(2):
-        total = lax.dot_general(
-            ones, total_ref[4 * k : 4 * k + 4].reshape(4 * COLS, LANES), (((1,), (1,)), ((), ())),
-            precision=lax.Precision.HIGHEST, preferred_element_type=F32,
-        )
-        send_ref[k : k + 1] = total[:1]
-    facts = jnp.where(valid(), recv_ref[8 * COLS :], own_ref[8 * COLS :])
+    facts = jnp.where(recv_ref[ROWS + 6 : ROWS + 7] > 0.5, recv_ref[ROWS:], own_ref[ROWS:])
     send_ref[2:3] = facts[4:5] + pltpu.roll(facts[5:6], 2, 1)
     send_ref[3:8] = jnp.zeros((5, LANES), F32)
-    first = 2 * jnp.bitwise_and(point, 3)
+    first = 2 * jnp.bitwise_and(point, 3) + 1
     for k in range(2):
         g = g_ref[first + k]
         elec, hole = g[:COLS], -sign * g[COLS:]
@@ -394,8 +393,8 @@
         name="fetch",
     )(*(pltpu.with_memory_space_constraint(x, pltpu.HBM) for x in inputs))
     both = lax.all_gather(right_side[0], "eh")
-    edge = lax.dynamic_slice_in_dim(both, jnp.where(low, BLK - 4, 0), 4, 1)
-    own = jnp.concatenate([edge.reshape(8 * COLS, LANES), facts], 0)
+    edge = lax.dynamic_slice_in_dim(both, jnp.where(low, BLK - EDGE, 0), EDGE, 1)
+    own = jnp.concatenate([edge.reshape(ROWS, LANES), facts], 0)
     recv = lax.ppermute(own, ALL, halo_pairs())
     hop_t, pair_t = pl.pallas_call(
         tables_kernel,
@@ -408,20 +407,20 @@
         compiler_params=VM,
         name="tables",
     )(hops, pairs)
-    win = lax.dynamic_slice_in_dim(both, jnp.where(low, 0, 6), 10, 1)
+    win = lax.dynamic_slice_in_dim(both, jnp.where(low, 0, BLK - INNER), INNER, 1)
     us, g, gs, acc = pl.pallas_call(
         inner_kernel,
         out_shape=[
-            jax.ShapeDtypeStruct((10, 6 * COLS, LANES), BF16),
-            jax.ShapeDtypeStruct((6, 2 * COLS, LANES), F32),
-            jax.ShapeDtypeStruct((6, 6 * COLS, LANES), BF16),
+            jax.ShapeDtypeStruct((INNER, 6 * COLS, LANES), BF16),
+            jax.ShapeDtypeStruct((INNER - 4, 2 * COLS, LANES), F32),
+            jax.ShapeDtypeStruct((INNER - 4, 6 * COLS, LANES), BF16),
             jax.ShapeDtypeStruct((8, 2 * COLS, LANES), F32),
         ],
         in_specs=[vmem] * 4,
         out_specs=[vmem] * 4,
         scratch_shapes=[
             pltpu.SMEM((8, LANES), F32),
-            pltpu.SMEM((8, 4), jnp.int32),
+            pltpu.SMEM((INNER, 4), jnp.int32),
             pltpu.SemaphoreType.DMA,
         ],
         compiler_params=VM,
@@ -433,21 +432,16 @@
             jax.ShapeDtypeStruct((72, LANES), F32),
             jax.ShapeDtypeStruct((2, COLS, LANES), F32),
         ],
-        in_specs=[vmem] * 10,
+        in_specs=[vmem] * 9,
         out_specs=[vmem] * 2,
         scratch_shapes=[
-            pltpu.VMEM((8, COLS, LANES), F32),
-            pltpu.VMEM((4, 6 * COLS, LANES), BF16),
+            pltpu.VMEM((EDGE, 6 * COLS, LANES), BF16),
             pltpu.VMEM((REACH, 2 * COLS, LANES), F32),
-            pltpu.VMEM((4, 6 * COLS, LANES), BF16),
-            pltpu.SMEM((8, LANES), F32),
-            pltpu.SMEM((8, LANES), F32),
-            pltpu.SMEM((WIN, 4), jnp.int32),
-            pltpu.SemaphoreType.DMA((2,)),
+            pltpu.VMEM((EDGE, 6 * COLS, LANES), BF16),
         ],
         compiler_params=VM,
         name="outer",
-    )(win, both, own, recv, hop_t, pair_t, us, g, gs, acc)
+    )(win, own, recv, hop_t, pair_t, us, g, gs, acc)
     sent = lax.all_gather(send, "eh")
     mom = jnp.concatenate([sent[0, :2] + sent[1, :2], sent[:, 2]], 0)
     mom = jnp.broadcast_to(mom[None], (DOMS, 4, LANES))

time: 48.2 us -> 47 us (0.975)
  Pallas kernels: 7.82 us -> 7.19 us
  blocking collectives: 36.1 us -> 35.5 us
    pallas_call x1, Pallas kernels: 2.22 us -> 1.38 us  [body(): pl.pallas_call(outer_kernel, out_shape=[jax.ShapeDtypeStruct((72, LANES),...]
    all_gather x1, blocking collectives: 2.92 us -> 2.24 us  [body(): sent = lax.all_gather(send, 'eh')]
  transfers between devices with their start and end apart: 1 -> 1, of which waited for: 0 -> 0; matrix products, arithmetic and copies ran while one was open for 0% -> 0% of each run, Pallas kernels for 6% -> 7%
where the time goes in v3:
time: 47 us; the launch traced here: 46.8 us
  blocking collectives  35.5 us (76%)
  Pallas kernels  7.19 us (15%)
  starting transfers between devices  4.01 us (9%)
    all_to_all x1, blocking collectives, body(): parts = lax.all_to_all(mom, 'dom', 0, 0)  30.9 us
    ppermute x1, starting transfers between devices, body(): recv = lax.ppermute(own, ALL, halo_pairs())  4.01 us
    all_gather x1, blocking collectives, body(): both = lax.all_gather(right_side[0], 'eh')  2.38 us
    pallas_call x1, Pallas kernels, body(): pl.pallas_call(inner_kernel, out_shape=[jax.ShapeDtypeStruct((INNER, 6 *...  2.35 us
    all_gather x1, blocking collectives, body(): sent = lax.all_gather(send, 'eh')  2.24 us
    pallas_call x1, Pallas kernels, body(): pl.pallas_call(outer_kernel, out_shape=[jax.ShapeDtypeStruct((72, LANES),...  1.38 us
    pallas_call x1, Pallas kernels, body(): pl.pallas_call(combine_kernel, out_shape=jax.ShapeDtypeStruct((1, 2, COLS...  1.33 us
    pallas_call x1, Pallas kernels, body(): pl.pallas_call(fetch_kernel, out_shape=[jax.ShapeDtypeStruct((8, LANES),...  1.23 us
  transfers between devices with their start and end apart: 1, of which 0 were waited for; matrix products, arithmetic and copies ran while one was open for 0% of the time, Pallas kernels for 7%

profile of v3, /device:TPU:24, one launch (start us, length us, event | category | flops | bytes accessed | tf_op | source)
XLA Modules:
  0.0 46.8 jit_solution(169405036613138978)
XLA Ops:
  0.0 2.4 %all_gather.9 = f32[2,16,32,128]{3,2,1,0:T(8,128)S(1)} all-gather(f32[1,16,32,128]{3,2,1,0:T(8,128)} %right_ref.1), channel_id=1, replica_groups=mesh['shift'=8,'dom'=32,'eh'=2] {'eh'}, dimensions={0}, use_global_device_ids=true | all-gather | bytes 786432 | tf_op jit(solution)/shard_map/all_gather | solution.py:395
  2.4 1.2 %fetch.1 = (f32[8,128]{1,0:T(8,128)S(1)}, f32[8,2,64,64]{3,2,1,0:T(8,128)S(1)}, f32[4,2,64,64]{3,2,1,0:T(8,128)S(1)}) custom-call(s32[3,16]{1,0:T(4,128)} %bitcast.12, s32[1,16]{1,0:T(1,128)} %bitcast.13, f32[1,2]{1,0:T(1,128)} %shift_ref.1, f32[1,2]{1,0:T(1,128)} %weight_ref.1, f32[8,2,64,64]{3,2,1,0:T(8,128)} %hop_ref.1, f32[4,2,64,64]{3,2,1,0:T(8,128)} %pair_ref.1), custom_call_target="tpu_custom_call" | custom-call | tf_op jit(solution)/shard_map/fetch/pallas_call | solution.py:376
  3.6 4.0 %collective-permute-start = (f32[200,128]{1,0:T(8,128)S(1)}, f32[200,128]{1,0:T(8,128)S(1)}, u32[]{:S(2)}, u32[]{:S(2)}) collective-permute-start(f32[200,128]{1,0:T(8,128)S(1)} %pad_maximum_fusion.own_ref), channel_id=1, source_target_pairs={{67,1},{128,2},{197,3},{258,4},{7,5},{4,6},{9,7},{6,8},{11,9},{8,1... | collective-permute-start | bytes 307208 | tf_op jit(solution)/shard_map/ppermute | solution.py:398
  7.7 0.9 %tables.1 = (bf16[24,128,384]{2,1,0:T(8,128)(2,1)S(1)}, bf16[8,128,384]{2,1,0:T(8,128)(2,1)S(1)}) custom-call(f32[8,2,64,64]{3,2,1,0:T(8,128)S(1)} %get-tuple-element.17.hop_ref, f32[4,2,64,64]{3,2,1,0:T(8,128)S(1)} %get-tuple-element.18.pair_ref), custom_call_target="tpu_custom_call" | custom-call | tf_op jit(solution)/shard_map/tables/pallas_call | solution.py:399
  8.6 2.4 %inner.1 = (bf16[11,192,128]{2,1,0:T(8,128)(2,1)S(1)}, f32[7,64,128]{2,1,0:T(8,128)S(1)}, bf16[7,192,128]{2,1,0:T(8,128)(2,1)S(1)}, f32[8,64,128]{2,1,0:T(8,128)S(1)}) custom-call(f32[2,11,32,128]{3,2,1,0:T(8,128)S(1)} %constant_dynamic-slice_fusion.1.win_ref, f32[200,128]{1,0:T(8,128)S(1)} %pad_maximum_fusion.own_ref, ...), custom_call_target="tpu_custom_call" | custom-call | tf_op jit(solution)/shard_map/inner/pallas_call | solution.py:411
  11.0 0.0 collective-permute-done.recv_ref
  11.0 0.0 copy-start
  11.0 1.4 %outer.1 = (f32[72,128]{1,0:T(8,128)S(1)}, f32[2,32,128]{2,1,0:T(8,128)S(1)}) custom-call(f32[2,11,32,128]{3,2,1,0:T(8,128)S(1)} %constant_dynamic-slice_fusion.1.win_ref, f32[200,128]{1,0:T(8,128)S(1)} %pad_maximum_fusion.own_ref, f32[200,128]{1,0:T(8,128)S(1)} %collective-permute-done.recv_ref, bf16[24,128,384]{2,1,0:T(8,128)(2,1)S(1)} %get-tuple-element.19.hop_t, ...), custom_call_target="tpu_custom_call" | custom-call | tf_op jit(solution)/shard_map/outer/pallas_call | solution.py:429
  12.4 2.2 %all-gather = f32[144,128]{1,0:T(8,128)S(1)} all-gather(f32[72,128]{1,0:T(8,128)S(1)} %get-tuple-element.25), channel_id=2, replica_groups=mesh['shift'=8,'dom'=32,'eh'=2] {'eh'}, dimensions={0}, use_global_device_ids=true | all-gather | bytes 110592 | tf_op jit(solution)/shard_map/all_gather | solution.py:445
  14.7 30.9 %all_to_all.5.mom_ref = f32[32,4,128]{2,1,0:T(4,128)S(1)} all-to-all(f32[32,4,128]{2,1,0:T(4,128)S(1)} %broadcast_in_dim.10), channel_id=1, replica_groups=mesh['shift'=8,'dom'=32,'eh'=2] {'dom'}, dimensions={0} | all-to-all | bytes 131072 | tf_op jit(solution)/shard_map/all_to_all | solution.py:448
  45.5 0.0 copy-done
  45.5 1.3 %combine.1 = f32[1,2,32,128]{3,2,1,0:T(8,128)} custom-call(f32[32,4,128]{2,1,0:T(4,128)S(1)} %all_to_all.5.mom_ref, f32[1,16,32,128]{3,2,1,0:T(8,128)S(1)} %copy-done, f32[2,32,128]{2,1,0:T(8,128)S(1)} %get-tuple-element.26.img_ref, f32[2,72,128]{2,1,0:T(8,128)S(1)} %bitcast.9), custom_call_target="tpu_custom_call" | custom-call | tf_op jit(solution)/shard_map/combine/pallas_call | solution.py:449
  (7 shorter events, 0.1 us)
Async XLA Ops:
  3.6 7.3 %collective-permute-start = (f32[200,128]{1,0:T(8,128)S(1)}, f32[200,128]{1,0:T(8,128)S(1)}, u32[]{:S(2)}, u32[]{:S(2)}) collective-permute-start(f32[200,128]{1,0:T(8,128)S(1)} %pad_maximum_fusion.own_ref), channel_id=1, source_target_pairs={{67,1},{128,2},{197,3},{258,4},{7,5},{4,6},{9,7},{6,8},{11,9},{8,1... | collective-permute-start | bytes 307208 | tf_op jit(solution)/shard_map/ppermute | solution.py:398
  11.0 34.5 %copy-start = (f32[1,16,32,128]{3,2,1,0:T(8,128)S(1)}, f32[1,16,32,128]{3,2,1,0:T(8,128)}, u32[]{:S(2)}) copy-start(f32[1,16,32,128]{3,2,1,0:T(8,128)} %right_ref.1) | copy-start | bytes 786436

commit v4 on v3

--- a/solution.py
+++ b/solution.py
@@ -131,8 +131,8 @@
 
 
 def fetch_kernel(
-    hop_s, pair_s, shift_ref, weight_ref, hop_ref, pair_ref,
-    facts_ref, hop_v, pair_v,
+    hop_s, pair_s, shift_ref, weight_ref, hop_ref, pair_ref, right_ref,
+    facts_ref, hop_v, pair_v, mine_ref,
     hop_k, pair_k, shift_v, weight_v, sem,
 ):
     copies = [
@@ -145,6 +145,7 @@
                 (weight_ref, weight_v),
                 (hop_ref, hop_v),
                 (pair_ref, pair_v),
+                (right_ref, mine_ref),
             )
         )
     ]
@@ -173,8 +174,13 @@
     facts.start()
     low = lax.axis_index("eh") == 0
     sign = halves((1, LANES))
+
+    def both(a):
+        x, y = win_ref[0, a], win_ref[1, a]
+        return jnp.where(low, x, y), jnp.where(low, y, x)
+
     for a in range(INNER):
-        us_ref[a] = parts_of(win_ref[0, a], win_ref[1, a], sign)
+        us_ref[a] = parts_of(*both(a), sign)
     facts.wait()
     for a in range(INNER - 2):
         for c in range(4):
@@ -185,7 +191,8 @@
         g = image([(us_ref, k + n) for n in range(5)], hop_t, pair_t, kinds)
         g_ref[k] = g
         gs_ref[k] = jnp.concatenate(split3(g), 0)
-        u = jnp.concatenate([win_ref[0, k + 2], win_ref[1, k + 2] * sign], 0)
+        elec, hole = both(k + 2)
+        u = jnp.concatenate([elec, hole * sign], 0)
         if k + 2 >= SPLIT:
             u, g = jnp.where(low, 0.0, u), jnp.where(low, 0.0, g)
         add_pairs(re, im, 0, u, u, swap(u))
@@ -208,9 +215,10 @@
     first = -1 if low else SPLIT
     sign = halves((1, LANES))
     edge = [-3, -2, -1] if low else [16, 17, 18]
+    e, h = (0, 1) if low else (1, 0)
     for n in range(EDGE):
-        elec = recv_ref[pl.ds(n * COLS, COLS)]
-        hole = recv_ref[pl.ds((EDGE + n) * COLS, COLS)]
+        elec = recv_ref[pl.ds((e * EDGE + n) * COLS, COLS)]
+        hole = recv_ref[pl.ds((h * EDGE + n) * COLS, COLS)]
         us_new[n] = parts_of(elec, hole, sign)
     for k in range(INNER - 4):
         g_ref[start + 2 + k - first] = g_in[k]
@@ -239,7 +247,7 @@
         g_ref[i - first] = g
         gs_new[n] = jnp.concatenate(split3(g), 0)
         if own:
-            u = jnp.concatenate([win_ref[0, i - start], win_ref[1, i - start] * sign], 0)
+            u = jnp.concatenate([win_ref[e, i - start], win_ref[h, i - start] * sign], 0)
             add_pairs(re, im, 0, u, u, swap(u))
             add_pairs(re, im, 1, u, g, swap(g))
             add_pairs(re, im, 2, g, g, swap(g))
@@ -292,7 +300,8 @@
     low = eh == 0
     sign = halves((1, LANES))
     facts = jnp.where(recv_ref[ROWS + 6 : ROWS + 7] > 0.5, recv_ref[ROWS:], own_ref[ROWS:])
-    send_ref[2:3] = facts[4:5] + pltpu.roll(facts[5:6], 2, 1)
+    params = facts[4:5] + pltpu.roll(facts[5:6], 2, 1)
+    send_ref[2:3] = jnp.where(low, params, pltpu.roll(params, 4, 1))
     send_ref[3:8] = jnp.zeros((5, LANES), F32)
     first = 2 * jnp.bitwise_and(point, 3) + 1
     for k in range(2):
@@ -312,12 +321,16 @@
 
 def cdiv(a, b):
     denom = jnp.maximum(b[0] * b[0] + b[1] * b[1], 1.0)
-    return (a[0] * b[0] + a[1] * b[1]) / denom, (a[1] * b[0] - a[0] * b[1]) / denom
+    scale = 1.0 / denom
+    return (a[0] * b[0] + a[1] * b[1]) * scale, (a[1] * b[0] - a[0] * b[1]) * scale
 
 
 def combine_kernel(mom_ref, right_ref, img_ref, sent_ref, out_ref):
-    total = jnp.sum(mom_ref[...], axis=0)
-    pts = jnp.concatenate([mom_ref[d, 2 + e : 3 + e] for d, e in POINT_AT], 0)
+    total = jnp.sum(mom_ref[:, :, : 2 * LANES], axis=0)
+    total = jnp.concatenate([total[:, :LANES], total[:, LANES:]], 0)
+    pts = [[mom_ref[d, :, 2 * LANES :] for d, e in POINT_AT if e == core] for core in range(EHS)]
+    pts = [jnp.concatenate(x, 0) for x in pts]
+    pts = jnp.concatenate([pts[0], pltpu.roll(pts[1], LANES - 4, 1)], 0)
 
     def moment(n):
         row = total[n // 2 : n // 2 + 1]
@@ -362,7 +375,7 @@
     holder = (point >= SHIFTS // 2).astype(jnp.int32)
     mine = lax.axis_index("eh") == holder
     for k in range(2):
-        b = right_ref[0, 2 * point + k]
+        b = right_ref[2 * point + k]
         g = jnp.where(mine, img_ref[k], sent_ref[holder, (1 + 4 * k) * 8 : (5 + 4 * k) * 8])
         out = cols[:, 0:1] * b + cols[:, 1:2] * (pltpu.roll(b, LANES // 2, 1) * sign)
         out = out + cols[:, 2:3] * g + cols[:, 3:4] * (pltpu.roll(g, LANES // 2, 1) * sign)
@@ -372,29 +385,33 @@
 def body(right_side, shifts, quad_weights, hop_table, pair_table, hop_type, pair_type):
     vmem = pl.BlockSpec(memory_space=pltpu.VMEM)
     low = lax.axis_index("eh") == 0
-    inputs = (hop_type.T, pair_type[None], shifts, quad_weights, hop_table, pair_table)
-    facts, hops, pairs = pl.pallas_call(
+    right = right_side[0]
+    inputs = (hop_type.T, pair_type[None], shifts, quad_weights, hop_table, pair_table, right)
+    other = lax.ppermute(right, "eh", [(0, 1), (1, 0)])
+    facts, hops, pairs, mine = pl.pallas_call(
         fetch_kernel,
         out_shape=[
             jax.ShapeDtypeStruct((8, LANES), F32),
             jax.ShapeDtypeStruct(hop_table.shape, F32),
             jax.ShapeDtypeStruct(pair_table.shape, F32),
-        ],
-        in_specs=[pl.BlockSpec(memory_space=pltpu.HBM)] * 6,
-        out_specs=[vmem] * 3,
+            jax.ShapeDtypeStruct(right.shape, F32),
+        ],
+        in_specs=[pl.BlockSpec(memory_space=pltpu.HBM)] * 7,
+        out_specs=[vmem] * 4,
         scratch_shapes=[
             pltpu.VMEM((3, BLK), jnp.int32),
             pltpu.VMEM((1, BLK), jnp.int32),
             pltpu.VMEM((1, 2), F32),
             pltpu.VMEM((1, 2), F32),
-            pltpu.SemaphoreType.DMA((6,)),
+            pltpu.SemaphoreType.DMA((7,)),
         ],
         compiler_params=VM,
         name="fetch",
     )(*(pltpu.with_memory_space_constraint(x, pltpu.HBM) for x in inputs))
-    both = lax.all_gather(right_side[0], "eh")
-    edge = lax.dynamic_slice_in_dim(both, jnp.where(low, BLK - EDGE, 0), EDGE, 1)
-    own = jnp.concatenate([edge.reshape(ROWS, LANES), facts], 0)
+    at = jnp.where(low, BLK - EDGE, 0)
+    edge = [lax.dynamic_slice_in_dim(x, at, EDGE, 0).reshape(-1, LANES) for x in (mine, other)]
+    own = jnp.concatenate([*edge, facts], 0)
+    own, hops, pairs = lax.optimization_barrier((own, hops, pairs))
     recv = lax.ppermute(own, ALL, halo_pairs())
     hop_t, pair_t = pl.pallas_call(
         tables_kernel,
@@ -407,7 +424,8 @@
         compiler_params=VM,
         name="tables",
     )(hops, pairs)
-    win = lax.dynamic_slice_in_dim(both, jnp.where(low, 0, BLK - INNER), INNER, 1)
+    at = jnp.where(low, 0, BLK - INNER)
+    win = jnp.stack([lax.dynamic_slice_in_dim(x, at, INNER, 0) for x in (mine, other)])
     us, g, gs, acc = pl.pallas_call(
         inner_kernel,
         out_shape=[
@@ -443,8 +461,8 @@
         name="outer",
     )(win, own, recv, hop_t, pair_t, us, g, gs, acc)
     sent = lax.all_gather(send, "eh")
-    mom = jnp.concatenate([sent[0, :2] + sent[1, :2], sent[:, 2]], 0)
-    mom = jnp.broadcast_to(mom[None], (DOMS, 4, LANES))
+    mom = (sent[0, :3] + sent[1, :3]).reshape(1, 1, 3 * LANES)
+    mom = jnp.broadcast_to(mom, (DOMS, 1, 3 * LANES))
     parts = lax.all_to_all(mom, "dom", 0, 0)
     return pl.pallas_call(
         combine_kernel,
@@ -453,7 +471,7 @@
         out_specs=vmem,
         compiler_params=VM,
         name="combine",
-    )(parts, right_side, img, sent)
+    )(parts, mine, img, sent)
 
 
 def solution(mesh):

time: 47 us -> 46.6 us (level)
  blocking collectives: 35.5 us -> 32.5 us
  starting transfers between devices: 4.01 us -> 5.92 us
    all_gather x1 -> x0, blocking collectives: 2.38 us -> none  [body(): both = lax.all_gather(right_side[0], 'eh')]
    ppermute x0 -> x1, starting transfers between devices: none -> 1.91 us  [body(): other = lax.ppermute(right, 'eh', [(0, 1), (1, 0)])]
    all_to_all x1, blocking collectives: 30.9 us -> 30.2 us  [body(): parts = lax.all_to_all(mom, 'dom', 0, 0)]
  transfers between devices with their start and end apart: 1 -> 2, of which waited for: 0 -> 1; matrix products, arithmetic and copies ran while one was open for 0% -> 0% of each run, Pallas kernels for 7% -> 10%
where the time goes in v4:
time: 46.6 us; the launch traced here: 46.4 us
  blocking collectives  32.5 us (70%)
  Pallas kernels  7.43 us (16%)
  starting transfers between devices  5.92 us (13%)
    all_to_all x1, blocking collectives, body(): parts = lax.all_to_all(mom, 'dom', 0, 0)  30.2 us
    ppermute x1, starting transfers between devices, body(): recv = lax.ppermute(own, ALL, halo_pairs())  4.01 us
    pallas_call x1, Pallas kernels, body(): pl.pallas_call(inner_kernel, out_shape=[jax.ShapeDtypeStruct((INNER, 6 *...  2.37 us
    all_gather x1, blocking collectives, body(): sent = lax.all_gather(send, 'eh')  2.28 us
    ppermute x1, starting transfers between devices, body(): other = lax.ppermute(right, 'eh', [(0, 1), (1, 0)])  1.91 us
    pallas_call x1, Pallas kernels, body(): pl.pallas_call(outer_kernel, out_shape=[jax.ShapeDtypeStruct((72, LANES),...  1.46 us
    pallas_call x1, Pallas kernels, body(): pl.pallas_call(combine_kernel, out_shape=jax.ShapeDtypeStruct((1, 2, COLS...  1.39 us
    pallas_call x1, Pallas kernels, body(): pl.pallas_call(fetch_kernel, out_shape=[jax.ShapeDtypeStruct((8, LANES),...  1.32 us
  transfers between devices with their start and end apart: 2, of which 1 were waited for; matrix products, arithmetic and copies ran while one was open for 0% of the time, Pallas kernels for 10%

profile of v4, /device:TPU:24, one launch (start us, length us, event | category | flops | bytes accessed | tf_op | source)
XLA Modules:
  0.0 46.4 jit_solution(2893358525452825645)
XLA Ops:
  0.0 1.9 %collective-permute-start = (f32[16,32,128]{2,1,0:T(8,128)}, f32[16,32,128]{2,1,0:T(8,128)S(1)}, u32[]{:S(2)}, u32[]{:S(2)}) collective-permute-start(f32[16,32,128]{2,1,0:T(8,128)} %bitcast.14), channel_id=1, source_target_pairs={{0,1},{1,0},{2,3},{3,2},{4,5},{5,4},{6,7},{7,6},{8,9},{9,8},{10,11... | collective-permute-start | bytes 786440 | tf_op jit(solution)/shard_map/ppermute | solution.py:390
  1.9 1.3 %fetch.1 = (f32[8,128]{1,0:T(8,128)S(1)}, f32[8,2,64,64]{3,2,1,0:T(8,128)S(1)}, f32[4,2,64,64]{3,2,1,0:T(8,128)S(1)}, f32[16,32,128]{2,1,0:T(8,128)S(1)}) custom-call(s32[3,16]{1,0:T(4,128)} %bitcast.18, s32[1,16]{1,0:T(1,128)} %bitcast.19, f32[1,2]{1,0:T(1,128)} %shift_ref.1, f32[1,2]{1,0:T(1,128)} %weight_ref.1, f32[8,2,64,64]{3,2,1,0:T(8,128)} %hop_ref.1, ...), custom_call_target="tpu_custom_call" | custom-call | tf_op jit(solution)/shard_map/fetch/pallas_call | solution.py:391
  3.3 0.3 collective-permute-done
  3.6 4.0 %collective-permute-start.1 = (f32[200,128]{1,0:T(8,128)S(1)}, f32[200,128]{1,0:T(8,128)S(1)}, u32[]{:S(2)}, u32[]{:S(2)}) collective-permute-start(f32[200,128]{1,0:T(8,128)S(1)} %pad_maximum_fusion.1.own_ref), channel_id=1, source_target_pairs={{67,1},{128,2},{197,3},{258,4},{7,5},{4,6},{9,7},{6,8},{11,9},{8,1... | collective-permute-start | bytes 307208 | tf_op jit(solution)/shard_map/ppermute | solution.py:415
  7.7 0.9 %tables.1 = (bf16[24,128,384]{2,1,0:T(8,128)(2,1)S(1)}, bf16[8,128,384]{2,1,0:T(8,128)(2,1)S(1)}) custom-call(f32[8,2,64,64]{3,2,1,0:T(8,128)S(1)} %get-tuple-element.25.hop_ref, f32[4,2,64,64]{3,2,1,0:T(8,128)S(1)} %get-tuple-element.26.pair_ref), custom_call_target="tpu_custom_call" | custom-call | tf_op jit(solution)/shard_map/tables/pallas_call | solution.py:416
  8.6 2.4 %inner.1 = (bf16[11,192,128]{2,1,0:T(8,128)(2,1)S(1)}, f32[7,64,128]{2,1,0:T(8,128)S(1)}, bf16[7,192,128]{2,1,0:T(8,128)(2,1)S(1)}, f32[8,64,128]{2,1,0:T(8,128)S(1)}) custom-call(f32[2,11,32,128]{3,2,1,0:T(8,128)S(1)} %pad_maximum_fusion.win_ref, f32[200,128]{1,0:T(8,128)S(1)} %pad_maximum_fusion.1.own_ref, ...), custom_call_target="tpu_custom_call" | custom-call | tf_op jit(solution)/shard_map/inner/pallas_call | solution.py:429
  11.0 0.0 collective-permute-done.1.recv_ref
  11.0 1.5 %outer.1 = (f32[72,128]{1,0:T(8,128)S(1)}, f32[2,32,128]{2,1,0:T(8,128)S(1)}) custom-call(f32[2,11,32,128]{3,2,1,0:T(8,128)S(1)} %pad_maximum_fusion.win_ref, f32[200,128]{1,0:T(8,128)S(1)} %pad_maximum_fusion.1.own_ref, f32[200,128]{1,0:T(8,128)S(1)} %collective-permute-done.1.recv_ref, bf16[24,128,384]{2,1,0:T(8,128)(2,1)S(1)} %get-tuple-element.27.hop_t, ...), custom_call_target="tpu_custom_call" | custom-call | tf_op jit(solution)/shard_map/outer/pallas_call | solution.py:447
  12.5 2.3 %all-gather = f32[144,128]{1,0:T(8,128)S(1)} all-gather(f32[72,128]{1,0:T(8,128)S(1)} %get-tuple-element.33), channel_id=2, replica_groups=mesh['shift'=8,'dom'=32,'eh'=2] {'eh'}, dimensions={0}, use_global_device_ids=true | all-gather | bytes 110592 | tf_op jit(solution)/shard_map/all_gather | solution.py:463
  14.8 30.2 %all_to_all.5.mom_ref = f32[32,1,384]{2,1,0:T(1,128)S(1)} all-to-all(f32[32,1,384]{2,1,0:T(1,128)S(1)} %broadcast_in_dim.9), channel_id=1, replica_groups=mesh['shift'=8,'dom'=32,'eh'=2] {'dom'}, dimensions={0} | all-to-all | bytes 98304 | tf_op jit(solution)/shard_map/all_to_all | solution.py:466
  45.0 1.4 %combine.1 = f32[1,2,32,128]{3,2,1,0:T(8,128)} custom-call(f32[32,1,384]{2,1,0:T(1,128)S(1)} %all_to_all.5.mom_ref, f32[16,32,128]{2,1,0:T(8,128)S(1)} %get-tuple-element.20.right_ref, f32[2,32,128]{2,1,0:T(8,128)S(1)} %get-tuple-element.34.img_ref, f32[2,72,128]{2,1,0:T(8,128)S(1)} %bitcast.13), custom_call_target="tpu_custom_call" | custom-call | tf_op jit(solution)/shard_map/combine/pallas_call | solution.py:467
  (8 shorter events, 0.1 us)
Async XLA Ops:
  0.0 3.6 %collective-permute-start = (f32[16,32,128]{2,1,0:T(8,128)}, f32[16,32,128]{2,1,0:T(8,128)S(1)}, u32[]{:S(2)}, u32[]{:S(2)}) collective-permute-start(f32[16,32,128]{2,1,0:T(8,128)} %bitcast.14), channel_id=1, source_target_pairs={{0,1},{1,0},{2,3},{3,2},{4,5},{5,4},{6,7},{7,6},{8,9},{9,8},{10,11... | collective-permute-start | bytes 786440 | tf_op jit(solution)/shard_map/ppermute | solution.py:390
  3.6 7.4 %collective-permute-start.1 = (f32[200,128]{1,0:T(8,128)S(1)}, f32[200,128]{1,0:T(8,128)S(1)}, u32[]{:S(2)}, u32[]{:S(2)}) collective-permute-start(f32[200,128]{1,0:T(8,128)S(1)} %pad_maximum_fusion.1.own_ref), channel_id=1, source_target_pairs={{67,1},{128,2},{197,3},{258,4},{7,5},{4,6},{9,7},{6,8},{11,9},{8,1... | collective-permute-start | bytes 307208 | tf_op jit(solution)/shard_map/ppermute | solution.py:415

commit v5 on v4

--- a/solution.py
+++ b/solution.py
@@ -22,7 +22,7 @@
     return (s * DOMS + d) * EHS + e
 
 
-TURNS = {(0, 1): 1, (1, 0): 2, (1, 1): 3, (2, 0): 4, (16, 1): 5, (17, 0): 6, (17, 1): 7}
+TURNS = {(1, 0): 1, (2, 0): 2, (3, 0): 3, (17, 0): 4, (18, 0): 5, (19, 0): 6, (4, 0): 7}
 POINT_AT = [(0, 0)] + list(TURNS)
 
 
@@ -300,8 +300,9 @@
     low = eh == 0
     sign = halves((1, LANES))
     facts = jnp.where(recv_ref[ROWS + 6 : ROWS + 7] > 0.5, recv_ref[ROWS:], own_ref[ROWS:])
-    params = facts[4:5] + pltpu.roll(facts[5:6], 2, 1)
-    send_ref[2:3] = jnp.where(low, params, pltpu.roll(params, 4, 1))
+    four = [facts[4:5, 0:1], facts[4:5, 1:2], facts[5:6, 0:1], facts[5:6, 1:2]]
+    params = jnp.concatenate([jnp.broadcast_to(x, (1, COLS)) for x in four], 1)
+    send_ref[2:3] = jnp.where(low, params, 0.0)
     send_ref[3:8] = jnp.zeros((5, LANES), F32)
     first = 2 * jnp.bitwise_and(point, 3) + 1
     for k in range(2):
@@ -325,28 +326,11 @@
     return (a[0] * b[0] + a[1] * b[1]) * scale, (a[1] * b[0] - a[0] * b[1]) * scale
 
 
-def combine_kernel(mom_ref, right_ref, img_ref, sent_ref, out_ref):
-    total = jnp.sum(mom_ref[:, :, : 2 * LANES], axis=0)
-    total = jnp.concatenate([total[:, :LANES], total[:, LANES:]], 0)
-    pts = [[mom_ref[d, :, 2 * LANES :] for d, e in POINT_AT if e == core] for core in range(EHS)]
-    pts = [jnp.concatenate(x, 0) for x in pts]
-    pts = jnp.concatenate([pts[0], pltpu.roll(pts[1], LANES - 4, 1)], 0)
-
-    def moment(n):
-        row = total[n // 2 : n // 2 + 1]
-        at = (n % 2) * 64
-        return tuple(
-            jnp.broadcast_to(row[:, at + k * COLS : at + (k + 1) * COLS], (SHIFTS, COLS))
-            for k in range(2)
-        )
-
-    def param(n):
-        return tuple(
-            jnp.broadcast_to(pts[:, n + k : n + k + 1], (SHIFTS, COLS)) for k in range(2)
-        )
-
-    m0, m1, m2, m3 = (moment(n) for n in range(4))
-    z, w = param(0), param(2)
+def coefficients(parts):
+    sums = jnp.sum(parts[:, : 2 * LANES], axis=0).reshape(4, 2, 1, COLS)
+    m0, m1, m2, m3 = ((sums[n, 0], sums[n, 1]) for n in range(4))
+    pts = jnp.concatenate([parts[d : d + 1, 2 * LANES :] for d, _ in POINT_AT], 0)
+    z, w = ((pts[:, k : k + COLS], pts[:, k + COLS : k + 2 * COLS]) for k in (0, 2 * COLS))
 
     def minus(a, b):
         return a[0] - b[0], a[1] - b[1]
@@ -366,10 +350,10 @@
     a1 = cdiv(rho, minus(cmul(z, pp), php))
     c0 = cmul(w, cadd(a0, cmul(a1, c)))
     c1 = cmul(w, cmul(a1, a0))
-    rows = [jnp.sum(x, axis=0, keepdims=True) for x in (*c0, *c1)]
-    stack = jnp.concatenate(rows + [jnp.zeros((4, COLS), F32)], 0)
-    stack = jnp.concatenate([stack, jnp.zeros((8, LANES - COLS), F32)], 1)
-    cols = stack.T[:COLS]
+    return jnp.stack([jnp.sum(x, axis=0) for x in (*c0, *c1)])
+
+
+def combine_kernel(coef_ref, right_ref, img_ref, sent_ref, out_ref):
     sign = -halves((1, LANES))
     point = lax.axis_index("shift")
     holder = (point >= SHIFTS // 2).astype(jnp.int32)
@@ -377,9 +361,8 @@
     for k in range(2):
         b = right_ref[2 * point + k]
         g = jnp.where(mine, img_ref[k], sent_ref[holder, (1 + 4 * k) * 8 : (5 + 4 * k) * 8])
-        out = cols[:, 0:1] * b + cols[:, 1:2] * (pltpu.roll(b, LANES // 2, 1) * sign)
-        out = out + cols[:, 2:3] * g + cols[:, 3:4] * (pltpu.roll(g, LANES // 2, 1) * sign)
-        out_ref[0, k] = out
+        out = coef_ref[0] * b + coef_ref[1] * (swap(b) * sign)
+        out_ref[0, k] = out + coef_ref[2] * g + coef_ref[3] * (swap(g) * sign)
 
 
 def body(right_side, shifts, quad_weights, hop_table, pair_table, hop_type, pair_type):
@@ -463,7 +446,9 @@
     sent = lax.all_gather(send, "eh")
     mom = (sent[0, :3] + sent[1, :3]).reshape(1, 1, 3 * LANES)
     mom = jnp.broadcast_to(mom, (DOMS, 1, 3 * LANES))
-    parts = lax.all_to_all(mom, "dom", 0, 0)
+    parts = lax.all_to_all(mom, "dom", 0, 0)[:, 0]
+    coef = coefficients(parts)[:, :, None]
+    coef = jnp.broadcast_to(coef, (4, COLS, LANES))
     return pl.pallas_call(
         combine_kernel,
         out_shape=jax.ShapeDtypeStruct((1, 2, COLS, LANES), F32),
@@ -471,7 +456,7 @@
         out_specs=vmem,
         compiler_params=VM,
         name="combine",
-    )(parts, mine, img, sent)
+    )(coef, mine, img, sent)
 
 
 def solution(mesh):

time: 46.6 us -> 46.5 us (level)
  blocking collectives: 32.5 us -> 30.2 us
  starting transfers between devices: 5.92 us -> 8.2 us
  Pallas kernels: 7.43 us -> 6.71 us
    ppermute x1, starting transfers between devices: 4.01 us -> 6.29 us  [body(): recv = lax.ppermute(own, ALL, halo_pairs())]
    all_to_all x1, blocking collectives: 30.2 us -> 28.3 us  [body(): parts = lax.all_to_all(mom, 'dom', 0, 0)[:, 0]]
    pallas_call x1, Pallas kernels: 1.39 us -> 0.72 us  [body(): pl.pallas_call(combine_kernel, out_shape=jax.ShapeDtypeStruct((1, 2, COLS...]
where the time goes in v5:
time: 46.5 us; the launch traced here: 46.3 us
  blocking collectives  30.2 us (65%)
  starting transfers between devices  8.2 us (18%)
  Pallas kernels  6.71 us (14%)
    all_to_all x1, blocking collectives, body(): parts = lax.all_to_all(mom, 'dom', 0, 0)[:, 0]  28.3 us
    ppermute x1, starting transfers between devices, body(): recv = lax.ppermute(own, ALL, halo_pairs())  6.29 us
    pallas_call x1, Pallas kernels, body(): pl.pallas_call(inner_kernel, out_shape=[jax.ShapeDtypeStruct((INNER, 6 *...  2.37 us
    ppermute x1, starting transfers between devices, body(): other = lax.ppermute(right, 'eh', [(0, 1), (1, 0)])  1.91 us
    all_gather x1, blocking collectives, body(): sent = lax.all_gather(send, 'eh')  1.85 us
    pallas_call x1, Pallas kernels, body(): pl.pallas_call(outer_kernel, out_shape=[jax.ShapeDtypeStruct((72, LANES),...  1.4 us
    pallas_call x1, Pallas kernels, body(): pl.pallas_call(fetch_kernel, out_shape=[jax.ShapeDtypeStruct((8, LANES),...  1.32 us
  transfers between devices with their start and end apart: 2, of which 1 were waited for; matrix products, arithmetic and copies ran while one was open for 0% of the time, Pallas kernels for 10%

profile of v5, /device:TPU:24, one launch (start us, length us, event | category | flops | bytes accessed | tf_op | source)
XLA Modules:
  0.0 46.3 jit_solution(5150318488226819996)
XLA Ops:
  0.0 1.9 %collective-permute-start = (f32[16,32,128]{2,1,0:T(8,128)}, f32[16,32,128]{2,1,0:T(8,128)S(1)}, u32[]{:S(2)}, u32[]{:S(2)}) collective-permute-start(f32[16,32,128]{2,1,0:T(8,128)} %bitcast.41), channel_id=1, source_target_pairs={{0,1},{1,0},{2,3},{3,2},{4,5},{5,4},{6,7},{7,6},{8,9},{9,8},{10,11... | collective-permute-start | bytes 786440 | tf_op jit(solution)/shard_map/ppermute | solution.py:373
  1.9 1.3 %fetch.1 = (f32[8,128]{1,0:T(8,128)S(1)}, f32[8,2,64,64]{3,2,1,0:T(8,128)S(1)}, f32[4,2,64,64]{3,2,1,0:T(8,128)S(1)}, f32[16,32,128]{2,1,0:T(8,128)S(1)}) custom-call(s32[3,16]{1,0:T(4,128)} %bitcast.49, s32[1,16]{1,0:T(1,128)} %bitcast.54, f32[1,2]{1,0:T(1,128)} %shift_ref.1, f32[1,2]{1,0:T(1,128)} %weight_ref.1, f32[8,2,64,64]{3,2,1,0:T(8,128)} %hop_ref.1, ...), custom_call_target="tpu_custom_call" | custom-call | tf_op jit(solution)/shard_map/fetch/pallas_call | solution.py:374
  3.3 0.3 collective-permute-done
  3.6 6.3 %collective-permute-start.1 = (f32[200,128]{1,0:T(8,128)S(1)}, f32[200,128]{1,0:T(8,128)S(1)}, u32[]{:S(2)}, u32[]{:S(2)}) collective-permute-start(f32[200,128]{1,0:T(8,128)S(1)} %pad_maximum_fusion.1.own_ref), channel_id=1, source_target_pairs={{3,1},{64,2},{5,3},{130,4},{7,5},{196,6},{9,7},{454,8},{11,9},{8,1... | collective-permute-start | bytes 307208 | tf_op jit(solution)/shard_map/ppermute | solution.py:398
  9.9 0.9 %tables.1 = (bf16[24,128,384]{2,1,0:T(8,128)(2,1)S(1)}, bf16[8,128,384]{2,1,0:T(8,128)(2,1)S(1)}) custom-call(f32[8,2,64,64]{3,2,1,0:T(8,128)S(1)} %get-tuple-element.25.hop_ref, f32[4,2,64,64]{3,2,1,0:T(8,128)S(1)} %get-tuple-element.26.pair_ref), custom_call_target="tpu_custom_call" | custom-call | tf_op jit(solution)/shard_map/tables/pallas_call | solution.py:399
  10.9 2.4 %inner.1 = (bf16[11,192,128]{2,1,0:T(8,128)(2,1)S(1)}, f32[7,64,128]{2,1,0:T(8,128)S(1)}, bf16[7,192,128]{2,1,0:T(8,128)(2,1)S(1)}, f32[8,64,128]{2,1,0:T(8,128)S(1)}) custom-call(f32[2,11,32,128]{3,2,1,0:T(8,128)S(1)} %pad_maximum_fusion.win_ref, f32[200,128]{1,0:T(8,128)S(1)} %pad_maximum_fusion.1.own_ref, ...), custom_call_target="tpu_custom_call" | custom-call | tf_op jit(solution)/shard_map/inner/pallas_call | solution.py:412
  13.3 0.0 collective-permute-done.1.recv_ref
  13.3 1.4 %outer.1 = (f32[72,128]{1,0:T(8,128)S(1)}, f32[2,32,128]{2,1,0:T(8,128)S(1)}) custom-call(f32[2,11,32,128]{3,2,1,0:T(8,128)S(1)} %pad_maximum_fusion.win_ref, f32[200,128]{1,0:T(8,128)S(1)} %pad_maximum_fusion.1.own_ref, f32[200,128]{1,0:T(8,128)S(1)} %collective-permute-done.1.recv_ref, bf16[24,128,384]{2,1,0:T(8,128)(2,1)S(1)} %get-tuple-element.27.hop_t, ...), custom_call_target="tpu_custom_call" | custom-call | tf_op jit(solution)/shard_map/outer/pallas_call | solution.py:430
  14.7 1.9 %all-gather = f32[144,128]{1,0:T(8,128)S(1)} all-gather(f32[72,128]{1,0:T(8,128)S(1)} %get-tuple-element.33), channel_id=2, replica_groups=mesh['shift'=8,'dom'=32,'eh'=2] {'eh'}, dimensions={0}, use_global_device_ids=true | all-gather | bytes 110592 | tf_op jit(solution)/shard_map/all_gather | solution.py:446
  16.6 28.3 %all_to_all.5 = f32[32,1,384]{2,1,0:T(1,128)S(1)} all-to-all(f32[32,1,384]{2,1,0:T(1,128)S(1)} %broadcast_in_dim.7), channel_id=1, replica_groups=mesh['shift'=8,'dom'=32,'eh'=2] {'dom'}, dimensions={0} | all-to-all | bytes 98304 | tf_op jit(solution)/shard_map/all_to_all | solution.py:449
  45.0 0.1 reshape.53
  45.1 0.1 multiply_subtract_fusion.5
  45.2 0.1 add_subtract_fusion.1
  45.3 0.1 multiply_add_fusion
  45.4 0.1 subtract_reduce_fusion.1
  45.5 0.1 broadcast_in_dim.16.coef_ref
  45.6 0.7 %combine.1 = f32[1,2,32,128]{3,2,1,0:T(8,128)} custom-call(f32[4,32,128]{2,1,0:T(8,128)S(1)} %broadcast_in_dim.16.coef_ref, f32[16,32,128]{2,1,0:T(8,128)S(1)} %get-tuple-element.20.right_ref, f32[2,32,128]{2,1,0:T(8,128)S(1)} %get-tuple-element.34.img_ref, f32[2,72,128]{2,1,0:T(8,128)S(1)} %bitcast.40), custom_call_target="tpu_custom_call" | custom-call | tf_op jit(solution)/shard_map/combine/pallas_call | solution.py:452
  (18 shorter events, 0.2 us)
Async XLA Ops:
  0.0 3.6 %collective-permute-start = (f32[16,32,128]{2,1,0:T(8,128)}, f32[16,32,128]{2,1,0:T(8,128)S(1)}, u32[]{:S(2)}, u32[]{:S(2)}) collective-permute-start(f32[16,32,128]{2,1,0:T(8,128)} %bitcast.41), channel_id=1, source_target_pairs={{0,1},{1,0},{2,3},{3,2},{4,5},{5,4},{6,7},{7,6},{8,9},{9,8},{10,11... | collective-permute-start | bytes 786440 | tf_op jit(solution)/shard_map/ppermute | solution.py:373
  3.6 9.6 %collective-permute-start.1 = (f32[200,128]{1,0:T(8,128)S(1)}, f32[200,128]{1,0:T(8,128)S(1)}, u32[]{:S(2)}, u32[]{:S(2)}) collective-permute-start(f32[200,128]{1,0:T(8,128)S(1)} %pad_maximum_fusion.1.own_ref), channel_id=1, source_target_pairs={{3,1},{64,2},{5,3},{130,4},{7,5},{196,6},{9,7},{454,8},{11,9},{8,1... | collective-permute-start | bytes 307208 | tf_op jit(solution)/shard_map/ppermute | solution.py:398

commit v6 on v5

--- a/solution.py
+++ b/solution.py
@@ -327,8 +327,9 @@
 
 
 def coefficients(parts):
-    sums = jnp.sum(parts[:, : 2 * LANES], axis=0).reshape(4, 2, 1, COLS)
-    m0, m1, m2, m3 = ((sums[n, 0], sums[n, 1]) for n in range(4))
+    sums = jnp.sum(parts[:, : 2 * LANES], axis=0, keepdims=True)
+    sums = [sums[:, k * COLS : (k + 1) * COLS] for k in range(8)]
+    m0, m1, m2, m3 = zip(sums[::2], sums[1::2])
     pts = jnp.concatenate([parts[d : d + 1, 2 * LANES :] for d, _ in POINT_AT], 0)
     z, w = ((pts[:, k : k + COLS], pts[:, k + COLS : k + 2 * COLS]) for k in (0, 2 * COLS))
 

time: 46.5 us -> 46.5 us (level)
  no operation moved by 1% of the time
where the time goes in v6:
time: 46.5 us; the launch traced here: 46.2 us
  blocking collectives  30.2 us (65%)
  starting transfers between devices  8.2 us (18%)
  Pallas kernels  6.7 us (14%)
  other arithmetic  0.53 us (1%)
    all_to_all x1, blocking collectives, body(): parts = lax.all_to_all(mom, 'dom', 0, 0)[:, 0]  28.3 us
    ppermute x1, starting transfers between devices, body(): recv = lax.ppermute(own, ALL, halo_pairs())  6.29 us
    pallas_call x1, Pallas kernels, body(): pl.pallas_call(inner_kernel, out_shape=[jax.ShapeDtypeStruct((INNER, 6 *...  2.37 us
    ppermute x1, starting transfers between devices, body(): other = lax.ppermute(right, 'eh', [(0, 1), (1, 0)])  1.91 us
    all_gather x1, blocking collectives, body(): sent = lax.all_gather(send, 'eh')  1.85 us
    pallas_call x1, Pallas kernels, body(): pl.pallas_call(outer_kernel, out_shape=[jax.ShapeDtypeStruct((72, LANES),...  1.4 us
    pallas_call x1, Pallas kernels, body(): pl.pallas_call(fetch_kernel, out_shape=[jax.ShapeDtypeStruct((8, LANES),...  1.32 us
  transfers between devices with their start and end apart: 2, of which 1 were waited for; matrix products, arithmetic and copies ran while one was open for 0% of the time, Pallas kernels for 10%

profile of v6, /device:TPU:24, one launch (start us, length us, event | category | flops | bytes accessed | tf_op | source)
XLA Modules:
  0.0 46.2 jit_solution(15409820604986860773)
XLA Ops:
  0.0 1.9 %collective-permute-start = (f32[16,32,128]{2,1,0:T(8,128)}, f32[16,32,128]{2,1,0:T(8,128)S(1)}, u32[]{:S(2)}, u32[]{:S(2)}) collective-permute-start(f32[16,32,128]{2,1,0:T(8,128)} %bitcast.40), channel_id=1, source_target_pairs={{0,1},{1,0},{2,3},{3,2},{4,5},{5,4},{6,7},{7,6},{8,9},{9,8},{10,11... | collective-permute-start | bytes 786440 | tf_op jit(solution)/shard_map/ppermute | solution.py:374
  1.9 1.3 %fetch.1 = (f32[8,128]{1,0:T(8,128)S(1)}, f32[8,2,64,64]{3,2,1,0:T(8,128)S(1)}, f32[4,2,64,64]{3,2,1,0:T(8,128)S(1)}, f32[16,32,128]{2,1,0:T(8,128)S(1)}) custom-call(s32[3,16]{1,0:T(4,128)} %bitcast.49, s32[1,16]{1,0:T(1,128)} %bitcast.54, f32[1,2]{1,0:T(1,128)} %shift_ref.1, f32[1,2]{1,0:T(1,128)} %weight_ref.1, f32[8,2,64,64]{3,2,1,0:T(8,128)} %hop_ref.1, ...), custom_call_target="tpu_custom_call" | custom-call | tf_op jit(solution)/shard_map/fetch/pallas_call | solution.py:375
  3.3 0.3 collective-permute-done
  3.6 6.3 %collective-permute-start.1 = (f32[200,128]{1,0:T(8,128)S(1)}, f32[200,128]{1,0:T(8,128)S(1)}, u32[]{:S(2)}, u32[]{:S(2)}) collective-permute-start(f32[200,128]{1,0:T(8,128)S(1)} %pad_maximum_fusion.1.own_ref), channel_id=1, source_target_pairs={{3,1},{64,2},{5,3},{130,4},{7,5},{196,6},{9,7},{454,8},{11,9},{8,1... | collective-permute-start | bytes 307208 | tf_op jit(solution)/shard_map/ppermute | solution.py:399
  9.9 0.9 %tables.1 = (bf16[24,128,384]{2,1,0:T(8,128)(2,1)S(1)}, bf16[8,128,384]{2,1,0:T(8,128)(2,1)S(1)}) custom-call(f32[8,2,64,64]{3,2,1,0:T(8,128)S(1)} %get-tuple-element.25.hop_ref, f32[4,2,64,64]{3,2,1,0:T(8,128)S(1)} %get-tuple-element.26.pair_ref), custom_call_target="tpu_custom_call" | custom-call | tf_op jit(solution)/shard_map/tables/pallas_call | solution.py:400
  10.9 2.4 %inner.1 = (bf16[11,192,128]{2,1,0:T(8,128)(2,1)S(1)}, f32[7,64,128]{2,1,0:T(8,128)S(1)}, bf16[7,192,128]{2,1,0:T(8,128)(2,1)S(1)}, f32[8,64,128]{2,1,0:T(8,128)S(1)}) custom-call(f32[2,11,32,128]{3,2,1,0:T(8,128)S(1)} %pad_maximum_fusion.win_ref, f32[200,128]{1,0:T(8,128)S(1)} %pad_maximum_fusion.1.own_ref, ...), custom_call_target="tpu_custom_call" | custom-call | tf_op jit(solution)/shard_map/inner/pallas_call | solution.py:413
  13.3 0.0 collective-permute-done.1.recv_ref
  13.3 1.4 %outer.1 = (f32[72,128]{1,0:T(8,128)S(1)}, f32[2,32,128]{2,1,0:T(8,128)S(1)}) custom-call(f32[2,11,32,128]{3,2,1,0:T(8,128)S(1)} %pad_maximum_fusion.win_ref, f32[200,128]{1,0:T(8,128)S(1)} %pad_maximum_fusion.1.own_ref, f32[200,128]{1,0:T(8,128)S(1)} %collective-permute-done.1.recv_ref, bf16[24,128,384]{2,1,0:T(8,128)(2,1)S(1)} %get-tuple-element.27.hop_t, ...), custom_call_target="tpu_custom_call" | custom-call | tf_op jit(solution)/shard_map/outer/pallas_call | solution.py:431
  14.7 1.9 %all-gather = f32[144,128]{1,0:T(8,128)S(1)} all-gather(f32[72,128]{1,0:T(8,128)S(1)} %get-tuple-element.33), channel_id=2, replica_groups=mesh['shift'=8,'dom'=32,'eh'=2] {'eh'}, dimensions={0}, use_global_device_ids=true | all-gather | bytes 110592 | tf_op jit(solution)/shard_map/all_gather | solution.py:447
  16.6 28.3 %all_to_all.5 = f32[32,1,384]{2,1,0:T(1,128)S(1)} all-to-all(f32[32,1,384]{2,1,0:T(1,128)S(1)} %broadcast_in_dim.18), channel_id=1, replica_groups=mesh['shift'=8,'dom'=32,'eh'=2] {'dom'}, dimensions={0} | all-to-all | bytes 98304 | tf_op jit(solution)/shard_map/all_to_all | solution.py:450
  45.0 0.1 divide_bitcast_fusion
  45.1 0.1 multiply_subtract_fusion.5
  45.2 0.1 add_subtract_fusion.1
  45.2 0.1 multiply_add_fusion
  45.3 0.1 subtract_reduce_fusion.1
  45.5 0.1 broadcast_in_dim.20.coef_ref
  45.5 0.7 %combine.1 = f32[1,2,32,128]{3,2,1,0:T(8,128)} custom-call(f32[4,32,128]{2,1,0:T(8,128)S(1)} %broadcast_in_dim.20.coef_ref, f32[16,32,128]{2,1,0:T(8,128)S(1)} %get-tuple-element.20.right_ref, f32[2,32,128]{2,1,0:T(8,128)S(1)} %get-tuple-element.34.img_ref, f32[2,72,128]{2,1,0:T(8,128)S(1)} %bitcast.39), custom_call_target="tpu_custom_call" | custom-call | tf_op jit(solution)/shard_map/combine/pallas_call | solution.py:453
  (16 shorter events, 0.2 us)
Async XLA Ops:
  0.0 3.6 %collective-permute-start = (f32[16,32,128]{2,1,0:T(8,128)}, f32[16,32,128]{2,1,0:T(8,128)S(1)}, u32[]{:S(2)}, u32[]{:S(2)}) collective-permute-start(f32[16,32,128]{2,1,0:T(8,128)} %bitcast.40), channel_id=1, source_target_pairs={{0,1},{1,0},{2,3},{3,2},{4,5},{5,4},{6,7},{7,6},{8,9},{9,8},{10,11... | collective-permute-start | bytes 786440 | tf_op jit(solution)/shard_map/ppermute | solution.py:374
  3.6 9.6 %collective-permute-start.1 = (f32[200,128]{1,0:T(8,128)S(1)}, f32[200,128]{1,0:T(8,128)S(1)}, u32[]{:S(2)}, u32[]{:S(2)}) collective-permute-start(f32[200,128]{1,0:T(8,128)S(1)} %pad_maximum_fusion.1.own_ref), channel_id=1, source_target_pairs={{3,1},{64,2},{5,3},{130,4},{7,5},{196,6},{9,7},{454,8},{11,9},{8,1... | collective-permute-start | bytes 307208 | tf_op jit(solution)/shard_map/ppermute | solution.py:399

commit v7 on v5

--- a/solution.py
+++ b/solution.py
@@ -168,11 +168,14 @@
 def inner_kernel(
     win_ref, own_ref, hop_t, pair_t,
     us_ref, g_ref, gs_ref, acc_ref,
-    own_s, kind_s, sem,
 ):
-    facts = pltpu.make_async_copy(own_ref.at[pl.ds(ROWS, 8)], own_s, sem)
-    facts.start()
     low = lax.axis_index("eh") == 0
+    own = kinds_row(own_ref[ROWS:])
+    own = [jnp.where(low, own[0, a], own[0, BLK - INNER + a]) for a in range(INNER - 2)]
+
+    def kind(a, c):
+        return jnp.bitwise_and(lax.shift_right_logical(own[a], 3 * c), 7)
+
     sign = halves((1, LANES))
 
     def both(a):
@@ -181,13 +184,9 @@
 
     for a in range(INNER):
         us_ref[a] = parts_of(*both(a), sign)
-    facts.wait()
-    for a in range(INNER - 2):
-        for c in range(4):
-            kind_s[a, c] = jnp.where(low, own_s[c, a], own_s[c, BLK - INNER + a]).astype(jnp.int32)
     re, im = [None] * 4, [None] * 4
     for k in range(INNER - 4):
-        kinds = [kind_s[k, 2], kind_s[k + 1, 1]] + [kind_s[k + 2, c] for c in range(4)]
+        kinds = [kind(k, 2), kind(k + 1, 1)] + [kind(k + 2, c) for c in range(4)]
         g = image([(us_ref, k + n) for n in range(5)], hop_t, pair_t, kinds)
         g_ref[k] = g
         gs_ref[k] = jnp.concatenate(split3(g), 0)
@@ -199,7 +198,7 @@
         add_pairs(re, im, 1, u, g, swap(g))
         add_pairs(re, im, 2, g, g, swap(g))
     for k in range(INNER - 6):
-        kinds = [kind_s[k + 2, c] for c in range(4)]
+        kinds = [kind(k + 2, c) for c in range(4)]
         y = forward_image([(gs_ref, k + n) for n in range(3)], hop_t, pair_t, kinds)
         add_pairs(re, im, 3, g_ref[k], y, swap(y))
     for n in range(4):
@@ -419,11 +418,6 @@
         ],
         in_specs=[vmem] * 4,
         out_specs=[vmem] * 4,
-        scratch_shapes=[
-            pltpu.SMEM((8, LANES), F32),
-            pltpu.SMEM((INNER, 4), jnp.int32),
-            pltpu.SemaphoreType.DMA,
-        ],
         compiler_params=VM,
         name="inner",
     )(win, own, hop_t, pair_t)

time: 46.5 us -> 46.5 us (level)
  blocking collectives: 30.2 us -> 30.7 us
  Pallas kernels: 6.71 us -> 6.22 us
    all_to_all x1, blocking collectives: 28.3 us -> 28.8 us  [body(): parts = lax.all_to_all(mom, 'dom', 0, 0)[:, 0]]
    pallas_call x1, Pallas kernels: 2.37 us -> 1.9 us  [body(): pl.pallas_call(inner_kernel, out_shape=[jax.ShapeDtypeStruct((INNER, 6 *...]
  transfers between devices with their start and end apart: 2 -> 2, of which waited for: 1 -> 1; matrix products, arithmetic and copies ran while one was open for 0% -> 0% of each run, Pallas kernels for 10% -> 9%
where the time goes in v7:
time: 46.5 us; the launch traced here: 46.3 us
  blocking collectives  30.7 us (66%)
  starting transfers between devices  8.2 us (18%)
  Pallas kernels  6.22 us (13%)
    all_to_all x1, blocking collectives, body(): parts = lax.all_to_all(mom, 'dom', 0, 0)[:, 0]  28.8 us
    ppermute x1, starting transfers between devices, body(): recv = lax.ppermute(own, ALL, halo_pairs())  6.29 us
    ppermute x1, starting transfers between devices, body(): other = lax.ppermute(right, 'eh', [(0, 1), (1, 0)])  1.91 us
    pallas_call x1, Pallas kernels, body(): pl.pallas_call(inner_kernel, out_shape=[jax.ShapeDtypeStruct((INNER, 6 *...  1.9 us
    all_gather x1, blocking collectives, body(): sent = lax.all_gather(send, 'eh')  1.85 us
    pallas_call x1, Pallas kernels, body(): pl.pallas_call(outer_kernel, out_shape=[jax.ShapeDtypeStruct((72, LANES),...  1.39 us
    pallas_call x1, Pallas kernels, body(): pl.pallas_call(fetch_kernel, out_shape=[jax.ShapeDtypeStruct((8, LANES),...  1.32 us
  transfers between devices with their start and end apart: 2, of which 1 were waited for; matrix products, arithmetic and copies ran while one was open for 0% of the time, Pallas kernels for 9%

profile of v7, /device:TPU:24, one launch (start us, length us, event | category | flops | bytes accessed | tf_op | source)
XLA Modules:
  0.0 46.3 jit_solution(17285087723715408849)
XLA Ops:
  0.0 1.9 %collective-permute-start = (f32[16,32,128]{2,1,0:T(8,128)}, f32[16,32,128]{2,1,0:T(8,128)S(1)}, u32[]{:S(2)}, u32[]{:S(2)}) collective-permute-start(f32[16,32,128]{2,1,0:T(8,128)} %bitcast.41), channel_id=1, source_target_pairs={{0,1},{1,0},{2,3},{3,2},{4,5},{5,4},{6,7},{7,6},{8,9},{9,8},{10,11... | collective-permute-start | bytes 786440 | tf_op jit(solution)/shard_map/ppermute | solution.py:372
  1.9 1.3 %fetch.1 = (f32[8,128]{1,0:T(8,128)S(1)}, f32[8,2,64,64]{3,2,1,0:T(8,128)S(1)}, f32[4,2,64,64]{3,2,1,0:T(8,128)S(1)}, f32[16,32,128]{2,1,0:T(8,128)S(1)}) custom-call(s32[3,16]{1,0:T(4,128)} %bitcast.49, s32[1,16]{1,0:T(1,128)} %bitcast.54, f32[1,2]{1,0:T(1,128)} %shift_ref.1, f32[1,2]{1,0:T(1,128)} %weight_ref.1, f32[8,2,64,64]{3,2,1,0:T(8,128)} %hop_ref.1, ...), custom_call_target="tpu_custom_call" | custom-call | tf_op jit(solution)/shard_map/fetch/pallas_call | solution.py:373
  3.3 0.3 collective-permute-done
  3.6 6.3 %collective-permute-start.1 = (f32[200,128]{1,0:T(8,128)S(1)}, f32[200,128]{1,0:T(8,128)S(1)}, u32[]{:S(2)}, u32[]{:S(2)}) collective-permute-start(f32[200,128]{1,0:T(8,128)S(1)} %pad_maximum_fusion.1.own_ref), channel_id=1, source_target_pairs={{3,1},{64,2},{5,3},{130,4},{7,5},{196,6},{9,7},{454,8},{11,9},{8,1... | collective-permute-start | bytes 307208 | tf_op jit(solution)/shard_map/ppermute | solution.py:397
  9.9 0.9 %tables.1 = (bf16[24,128,384]{2,1,0:T(8,128)(2,1)S(1)}, bf16[8,128,384]{2,1,0:T(8,128)(2,1)S(1)}) custom-call(f32[8,2,64,64]{3,2,1,0:T(8,128)S(1)} %get-tuple-element.25.hop_ref, f32[4,2,64,64]{3,2,1,0:T(8,128)S(1)} %get-tuple-element.26.pair_ref), custom_call_target="tpu_custom_call" | custom-call | tf_op jit(solution)/shard_map/tables/pallas_call | solution.py:398
  10.9 1.9 %inner.1 = (bf16[11,192,128]{2,1,0:T(8,128)(2,1)S(1)}, f32[7,64,128]{2,1,0:T(8,128)S(1)}, bf16[7,192,128]{2,1,0:T(8,128)(2,1)S(1)}, f32[8,64,128]{2,1,0:T(8,128)S(1)}) custom-call(f32[2,11,32,128]{3,2,1,0:T(8,128)S(1)} %pad_maximum_fusion.win_ref, f32[200,128]{1,0:T(8,128)S(1)} %pad_maximum_fusion.1.own_ref, ...), custom_call_target="tpu_custom_call" | custom-call | tf_op jit(solution)/shard_map/inner/pallas_call | solution.py:411
  12.8 0.0 collective-permute-done.1.recv_ref
  12.8 1.4 %outer.1 = (f32[72,128]{1,0:T(8,128)S(1)}, f32[2,32,128]{2,1,0:T(8,128)S(1)}) custom-call(f32[2,11,32,128]{3,2,1,0:T(8,128)S(1)} %pad_maximum_fusion.win_ref, f32[200,128]{1,0:T(8,128)S(1)} %pad_maximum_fusion.1.own_ref, f32[200,128]{1,0:T(8,128)S(1)} %collective-permute-done.1.recv_ref, bf16[24,128,384]{2,1,0:T(8,128)(2,1)S(1)} %get-tuple-element.27.hop_t, ...), custom_call_target="tpu_custom_call" | custom-call | tf_op jit(solution)/shard_map/outer/pallas_call | solution.py:424
  14.2 1.9 %all-gather = f32[144,128]{1,0:T(8,128)S(1)} all-gather(f32[72,128]{1,0:T(8,128)S(1)} %get-tuple-element.33), channel_id=2, replica_groups=mesh['shift'=8,'dom'=32,'eh'=2] {'eh'}, dimensions={0}, use_global_device_ids=true | all-gather | bytes 110592 | tf_op jit(solution)/shard_map/all_gather | solution.py:440
  16.1 28.8 %all_to_all.5 = f32[32,1,384]{2,1,0:T(1,128)S(1)} all-to-all(f32[32,1,384]{2,1,0:T(1,128)S(1)} %broadcast_in_dim.7), channel_id=1, replica_groups=mesh['shift'=8,'dom'=32,'eh'=2] {'dom'}, dimensions={0} | all-to-all | bytes 98304 | tf_op jit(solution)/shard_map/all_to_all | solution.py:443
  45.0 0.1 reshape.53
  45.1 0.1 multiply_subtract_fusion.5
  45.2 0.1 add_subtract_fusion.1
  45.3 0.1 multiply_add_fusion
  45.4 0.1 subtract_reduce_fusion.1
  45.5 0.1 broadcast_in_dim.16.coef_ref
  45.6 0.7 %combine.1 = f32[1,2,32,128]{3,2,1,0:T(8,128)} custom-call(f32[4,32,128]{2,1,0:T(8,128)S(1)} %broadcast_in_dim.16.coef_ref, f32[16,32,128]{2,1,0:T(8,128)S(1)} %get-tuple-element.20.right_ref, f32[2,32,128]{2,1,0:T(8,128)S(1)} %get-tuple-element.34.img_ref, f32[2,72,128]{2,1,0:T(8,128)S(1)} %bitcast.40), custom_call_target="tpu_custom_call" | custom-call | tf_op jit(solution)/shard_map/combine/pallas_call | solution.py:446
  (18 shorter events, 0.2 us)
Async XLA Ops:
  0.0 3.6 %collective-permute-start = (f32[16,32,128]{2,1,0:T(8,128)}, f32[16,32,128]{2,1,0:T(8,128)S(1)}, u32[]{:S(2)}, u32[]{:S(2)}) collective-permute-start(f32[16,32,128]{2,1,0:T(8,128)} %bitcast.41), channel_id=1, source_target_pairs={{0,1},{1,0},{2,3},{3,2},{4,5},{5,4},{6,7},{7,6},{8,9},{9,8},{10,11... | collective-permute-start | bytes 786440 | tf_op jit(solution)/shard_map/ppermute | solution.py:372
  3.6 9.2 %collective-permute-start.1 = (f32[200,128]{1,0:T(8,128)S(1)}, f32[200,128]{1,0:T(8,128)S(1)}, u32[]{:S(2)}, u32[]{:S(2)}) collective-permute-start(f32[200,128]{1,0:T(8,128)S(1)} %pad_maximum_fusion.1.own_ref), channel_id=1, source_target_pairs={{3,1},{64,2},{5,3},{130,4},{7,5},{196,6},{9,7},{454,8},{11,9},{8,1... | collective-permute-start | bytes 307208 | tf_op jit(solution)/shard_map/ppermute | solution.py:397
